TPU v7x, 256 devices: a whole 4x4x8 slice. The times are simulated.
256 devices in a mesh: section: 32 (over z_hi, x, core), tensor: 8 (over z_lo, y).
Axes of the slice: x: 4, y: 4, z: 8 (z_hi: 4, z_lo: 2; z = z_hi * 2 + z_lo), core: 2. Of those that a mesh axis runs over, the one named last changes fastest.
Arguments:
- acts: bfloat16 [32, 512, 4096], P('section', 'tensor'), may hold values from -6 to 6
- next_grad: bfloat16 [32, 512, 4096], P('section', 'tensor'), may hold values from -6 to 6
- head_grad: bfloat16 [512, 4096], P('tensor'), may hold values from -6 to 6
- blocks: bfloat16 [32, 768, 12288], P('section', 'tensor'), may hold values from -0.875 to 0.875
- block_row: int32 [32, 768], P('section', 'tensor'), may hold values from 0 to 63, as said below
- block_col: int32 [32, 768], P('section', 'tensor'), may hold values from 0 to 55, as said below
- live: int32 [32, 8], P('section', 'tensor'), may hold values from 12 to 96, as said below
Outputs:
- input_grad: bfloat16 [32, 512, 4096], P('section', 'tensor')
- block_grads: bfloat16 [32, 768, 12288], P('section', 'tensor')
Inputs may be any that keep to these rules, and one draw needn't show every extreme that they name: `block_row`: within one shard of one section the live slots name distinct blocks. `block_col`: within one shard of one section the live slots name distinct blocks. Every section has a shard with all 96 slots live.
All inputs are finite; a program needn't handle non-finite values.
Results may differ from a plain program's by a relative error of at most 0.023.
Values may be sent and summed in bfloat16 or wider, within the bound.
A program may use at most 192 MiB of HBM per device.

v0:
```python
import jax
import jax.numpy as jnp
from jax import lax
from jax.sharding import PartitionSpec as P

FF = 28672


def shifted(block, axis, distance):
    devices = range(lax.axis_size(axis))
    route = [((i - distance) % len(devices), i) for i in devices]
    return lax.ppermute(block, axis, route)


def spread(per_slot, hot_table, form):
    high_part = per_slot.astype(jnp.bfloat16)
    low_part = (per_slot - high_part.astype(jnp.float32)).astype(jnp.bfloat16)
    first = jnp.einsum(form, high_part, hot_table, preferred_element_type=jnp.float32)
    return first + jnp.einsum(form, low_part, hot_table, preferred_element_type=jnp.float32)


def per_device(acts, next_grad, head_grad, blocks, block_row, block_col, live):
    at_front = lax.axis_index("section") == 0
    payload = jnp.where(at_front, head_grad[None], next_grad)
    shard_rows = acts.shape[1]
    model_width = acts.shape[2]
    gathered = lax.all_gather(payload, "tensor", axis=1, tiled=True)
    incoming_all = shifted(gathered, "section", -1)
    incoming = lax.dynamic_slice_in_dim(
        incoming_all, lax.axis_index("tensor") * shard_rows, shard_rows, 1
    )
    acts_all = lax.all_gather(acts, "tensor", axis=1, tiled=True)
    tokens = acts_all.shape[1]
    row_count = model_width // 64
    col_count = FF // lax.axis_size("tensor") // 64
    capacity = blocks.shape[1]
    act_blocks = acts_all[0].reshape(tokens, row_count, 64)
    grad_blocks = incoming_all[0].reshape(tokens, row_count, 64)
    row_ids = block_row[0]
    col_ids = block_col[0]
    is_live = jnp.arange(capacity) < live[0, 0]
    weights = jnp.where(is_live[:, None], blocks[0], jnp.zeros_like(blocks[0])).reshape(
        capacity, 3, 64, 64
    )
    w_gate = weights[:, 0]
    w_up = weights[:, 1]
    w_down = weights[:, 2]
    x_slot = jnp.take(act_blocks, row_ids, axis=1)
    dy_slot = jnp.take(grad_blocks, row_ids, axis=1)
    col_hot = (col_ids[:, None] == jnp.arange(col_count)[None, :]).astype(jnp.bfloat16)
    row_hot = (row_ids[:, None] == jnp.arange(row_count)[None, :]).astype(jnp.bfloat16)
    gate = spread(
        jnp.einsum("tkd,kdf->tkf", x_slot, w_gate, preferred_element_type=jnp.float32),
        col_hot,
        "tkf,kc->tcf",
    )
    upper = spread(
        jnp.einsum("tkd,kdf->tkf", x_slot, w_up, preferred_element_type=jnp.float32),
        col_hot,
        "tkf,kc->tcf",
    )
    hidden_grad = spread(
        jnp.einsum("tkd,kfd->tkf", dy_slot, w_down, preferred_element_type=jnp.float32),
        col_hot,
        "tkf,kc->tcf",
    )
    sigmoid_gate = jax.nn.sigmoid(gate)
    activated = gate * sigmoid_gate
    hidden = (activated * upper).astype(jnp.bfloat16)
    gate_grad = (hidden_grad * upper * sigmoid_gate * (1.0 + gate * (1.0 - sigmoid_gate))).astype(
        jnp.bfloat16
    )
    up_grad = (hidden_grad * activated).astype(jnp.bfloat16)
    g_slot = jnp.take(gate_grad, col_ids, axis=1)
    u_slot = jnp.take(up_grad, col_ids, axis=1)
    h_slot = jnp.take(hidden, col_ids, axis=1)
    back_slot = jnp.einsum("tkf,kdf->tkd", g_slot, w_gate, preferred_element_type=jnp.float32)
    back_slot = back_slot + jnp.einsum(
        "tkf,kdf->tkd", u_slot, w_up, preferred_element_type=jnp.float32
    )
    placed = spread(back_slot, row_hot, "tkd,kr->trd")
    summed = lax.psum_scatter(
        placed.reshape(lax.axis_size("tensor") * shard_rows, model_width).astype(jnp.bfloat16),
        "tensor",
        scatter_dimension=0,
        tiled=True,
    ).astype(jnp.float32)
    input_grad = (incoming[0].astype(jnp.float32) + summed).astype(jnp.bfloat16)[None]
    grad_gate = jnp.einsum("tkd,tkf->kdf", x_slot, g_slot, preferred_element_type=jnp.float32)
    grad_up = jnp.einsum("tkd,tkf->kdf", x_slot, u_slot, preferred_element_type=jnp.float32)
    grad_down = jnp.einsum("tkf,tkd->kfd", h_slot, dy_slot, preferred_element_type=jnp.float32)
    stacked = (
        jnp.stack([grad_gate, grad_up, grad_down], axis=1)
        * is_live.astype(jnp.float32)[:, None, None, None]
    )
    block_grads = stacked.reshape(1, capacity, 12288).astype(jnp.bfloat16)
    return (input_grad, block_grads)


def solution(mesh):
    return jax.shard_map(
        per_device,
        mesh=mesh,
        in_specs=(
            P("section", "tensor", None),
            P("section", "tensor", None),
            P("tensor", None),
            P("section", "tensor", None),
            P("section", "tensor"),
            P("section", "tensor"),
            P("section", "tensor"),
        ),
        out_specs=(P("section", "tensor", None), P("section", "tensor", None)),
        check_vma=False,
    )
```

profile of v0, /device:TPU:64, one launch (start us, length us, event | category | flops | bytes accessed | tf_op | source)
XLA Modules:
  0.0 456.5 jit_solution(11317155966660130684)
XLA Ops:
  7.2 0.0 all-gather.3.cloned.1.call-start
  7.2 2.1 bitcast_select_fusion
  9.3 0.0 all-gather.3.cloned.1.call-update
  9.3 0.0 all-gather.5.cloned.1.call-start
  9.3 0.7 all-gather.5.cloned.1.call-update
  10.0 0.0 reduce-scatter.4.cloned.1.call-start
  10.7 0.0 copy-start.4
  10.8 3.3 copy.47
  14.1 0.0 copy-start.3
  14.1 7.4 %copy.48 = bf16[96,3,64,64]{3,2,0,1:T(8,128)(2,1)} copy(bf16[96,3,64,64]{0,3,2,1:T(8,128)(2,1)S(1)} %bitcast.184) | data formatting | bytes 4718592 | tf_op jit(solution)/shard_map/squeeze | solution.py:42
  21.5 0.0 copy-done.4
  21.5 46.3 %all-gather.3.cloned.1.call-done = bf16[1,512,4096]{2,1,0:T(8,128)(2,1)} async-done(((bf16[1,64,4096]{2,1,0:T(8,128)(2,1)}), bf16[1,512,4096]{2,1,0:T(8,128)(2,1)}) %all-gather.3.cloned.1.call-update) | async-done | bytes 4194320 | tf_op jit(solution)/shard_map/all_gather | solution.py:27
  67.9 6.5 %copy.46 = bf16[1,512,4096]{1,2,0:T(8,128)(2,1)} copy(bf16[1,512,4096]{2,1,0:T(8,128)(2,1)} %all-gather.3.cloned.1.call-done) | data formatting | bytes 8388608 | tf_op jit(solution)/shard_map/all_gather | solution.py:27
  74.4 1.9 collective-permute-start
  76.3 0.0 copy-done.3
  76.3 4.9 %broadcast_select_fusion.4 = bf16[96,3,64,64]{3,2,0,1:T(8,128)(2,1)} fusion(bf16[96,3,64,64]{3,2,0,1:T(8,128)(2,1)} %copy.48, pred[96]{0:T(512)(128)(4,1)S(1)} %iota_compare_fusion.2), kind=kLoop, calls=%fused_computation.76 | loop fusion | flops 1179648 | bytes 4718688 | tf_op jit(solution)/shard_map/jit(_where)/select_n | solution.py:42
  81.2 106.2 %all-gather.5.cloned.1.call-done = bf16[1,512,4096]{2,1,0:T(8,128)(2,1)} async-done(((bf16[1,64,4096]{2,1,0:T(8,128)(2,1)}), bf16[1,512,4096]{2,1,0:T(8,128)(2,1)}) %all-gather.5.cloned.1.call-update) | async-done | bytes 4194320 | tf_op jit(solution)/shard_map/all_gather | solution.py:32
  187.4 6.6 %copy.51 = bf16[1,512,4096]{1,2,0:T(8,128)(2,1)} copy(bf16[1,512,4096]{2,1,0:T(8,128)(2,1)} %all-gather.5.cloned.1.call-done) | data formatting | bytes 8388608 | tf_op jit(solution)/shard_map/all_gather | solution.py:32
  194.0 8.4 %gather_fusion.1 = bf16[96,512,64]{1,2,0:T(8,128)(2,1)} fusion(bf16[512,64,64]{0,2,1:T(8,128)(2,1)} %bitcast.177, s32[1024]{0:T(1024)S(1)} %pad_clamp_fusion.1), kind=kCustom, calls=%fused_computation.2.clone | custom fusion | bytes 12583296 | tf_op jit(solution)/shard_map/jit(_take)/gather | solution.py:48
  202.4 7.8 %fusion.1 = (bf16[512,96,64]{0,2,1:T(8,128)(2,1)}, bf16[512,96,64]{0,2,1:T(8,128)(2,1)S(1)}) fusion(bf16[96,512,64]{1,2,0:T(8,128)(2,1)} %gather_fusion.1, pred[96]{0:T(512)(128)(4,1)S(1)} %get-tuple-element.20, bf16[96,3,64,64]{3,2,0,1:T(8,128)(2,1)} %broadcast_select_fusion.4), kind=kOutput, calls=%fused_computation.10 | convolution fusion | flops 418381824 | bytes 20447328 | tf_op jit(solution)/shard_map/tkd,kdf->tkf/dot_general | solution.py:53
  210.2 0.0 slice-start
  210.2 13.5 %fusion.36 = f32[56,512,64]{1,0,2:T(8,128)} fusion(bf16[512,96,64]{0,2,1:T(8,128)(2,1)} %get-tuple-element.12, s32[96]{0:T(128)S(1)} %bitcast.185), kind=kOutput, calls=%fused_computation.57 | convolution fusion | flops 352326912 | bytes 13631872 | tf_op jit(solution)/shard_map/tkf,kc->tcf/dot_general | solution.py:19
  223.7 11.0 %fusion.38 = f32[56,512,64]{1,0,2:T(8,128)} fusion(bf16[512,96,64]{0,2,1:T(8,128)(2,1)S(1)} %get-tuple-element.13, s32[96]{0:T(128)S(1)} %bitcast.186), kind=kOutput, calls=%fused_computation.59 | convolution fusion | flops 352326912 | bytes 13631872 | tf_op jit(solution)/shard_map/tkf,kc->tcf/dot_general | solution.py:18
  234.7 0.0 slice-done
  234.7 0.0 slice-done.1
  234.7 5.5 %fusion.2 = (bf16[512,96,64]{0,2,1:T(8,128)(2,1)S(1)}, bf16[512,96,64]{0,2,1:T(8,128)(2,1)}) fusion(bf16[96,512,64]{1,2,0:T(8,128)(2,1)S(1)} %bitcast.176, pred[96]{0:T(512)(128)(4,1)S(1)} %get-tuple-element.20, bf16[96,3,64,64]{3,2,0,1:T(8,128)(2,1)} %broadcast_select_fusion.4), kind=kOutput, calls=%fused_computation.13 | convolution fusion | flops 418381824 | bytes 20447328 | tf_op jit(solution)/shard_map/tkd,kdf->tkf/dot_general | solution.py:58
  240.3 10.5 %fusion.40 = f32[56,512,64]{1,0,2:T(8,128)} fusion(bf16[512,96,64]{0,2,1:T(8,128)(2,1)S(1)} %get-tuple-element.10, s32[96]{0:T(128)S(1)} %bitcast.187), kind=kOutput, calls=%fused_computation.61 | convolution fusion | flops 352326912 | bytes 13631872 | tf_op jit(solution)/shard_map/tkf,kc->tcf/dot_general | solution.py:19
  250.8 0.0 collective-permute-done
  250.8 8.3 %gather_fusion = bf16[96,512,64]{1,2,0:T(8,128)(2,1)} fusion(bf16[512,64,64]{0,2,1:T(8,128)(2,1)} %bitcast.10, s32[1024]{0:T(1024)S(1)} %pad_clamp_fusion.1), kind=kCustom, calls=%fused_computation.clone | custom fusion | bytes 12583296 | tf_op jit(solution)/shard_map/jit(_take)/gather | solution.py:49
  259.1 5.1 %fusion.3 = (bf16[512,96,64]{0,2,1:T(8,128)(2,1)S(1)}, bf16[512,96,64]{0,2,1:T(8,128)(2,1)S(1)}) fusion(bf16[96,512,64]{1,2,0:T(8,128)(2,1)} %gather_fusion, pred[96]{0:T(512)(128)(4,1)S(1)} %get-tuple-element.20, bf16[96,3,64,64]{3,2,0,1:T(8,128)(2,1)} %broadcast_select_fusion.4), kind=kOutput, calls=%fused_computation.16 | convolution fusion | flops 418381824 | bytes 20447328 | tf_op jit(solution)/shard_map/tkd,kfd->tkf/dot_general | solution.py:63
  264.2 10.6 %fusion.44 = f32[56,512,64]{1,0,2:T(8,128)} fusion(bf16[512,96,64]{0,2,1:T(8,128)(2,1)S(1)} %get-tuple-element.8, s32[96]{0:T(128)S(1)} %bitcast.188), kind=kOutput, calls=%fused_computation.65 | convolution fusion | flops 352326912 | bytes 13631872 | tf_op jit(solution)/shard_map/tkf,kc->tcf/dot_general | solution.py:19
  274.8 10.9 %fusion.46 = f32[56,512,64]{1,0,2:T(8,128)} fusion(bf16[512,96,64]{0,2,1:T(8,128)(2,1)S(1)} %get-tuple-element.9, s32[96]{0:T(128)S(1)} %bitcast.189), kind=kOutput, calls=%fused_computation.67 | convolution fusion | flops 352326912 | bytes 13631872 | tf_op jit(solution)/shard_map/tkf,kc->tcf/dot_general | solution.py:18
  285.7 21.7 %fusion.11 = (bf16[512,56,64]{0,1,2:T(8,128)(2,1)}, bf16[512,56,64]{0,1,2:T(8,128)(2,1)}, bf16[512,56,64]{0,1,2:T(8,128)(2,1)}) fusion(f32[56,512,64]{1,0,2:T(8,128)} %fusion.40, f32[56,512,64]{1,0,2:T(8,128)} %fusion.38, f32[56,512,64]{1,0,2:T(8,128)} %fusion.36, f32[56,512,64]{1,0,2:T(8,128)} %fusion.46, f32[56,512,64]{1,0,2:T(8,128)} %fusion.44, ...), kind=kOutput, calls=%fused_computation.31 | convolution fusion | flops 385357056 | bytes 54002048 | tf_op jit(solution)/shard_map/tkf,kc->tcf/dot_general | solution.py:18
  307.5 5.2 %copy.58 = bf16[512,56,64]{0,2,1:T(8,128)(2,1)} copy(bf16[512,56,64]{0,1,2:T(8,128)(2,1)} %get-tuple-element.15) | data formatting | bytes 7340032 | tf_op jit(solution)/shard_map/convert_element_type | solution.py:70
  312.7 0.0 copy-done.2
  312.7 3.1 copy.59
  315.8 8.1 %gather_fusion.2 = bf16[96,512,64]{1,2,0:T(8,128)(2,1)} fusion(bf16[512,56,64]{0,2,1:T(8,128)(2,1)} %copy.58, s32[1024]{0:T(1024)S(1)} %pad_clamp_fusion), kind=kCustom, calls=%fused_computation.1.clone | custom fusion | bytes 12583296 | tf_op jit(solution)/shard_map/jit(_take)/gather | solution.py:74
  323.9 8.1 %gather_fusion.3 = bf16[96,512,64]{1,2,0:T(8,128)(2,1)} fusion(bf16[512,56,64]{0,2,1:T(8,128)(2,1)} %copy.59, s32[1024]{0:T(1024)S(1)} %pad_clamp_fusion), kind=kCustom, calls=%fused_computation.3.clone | custom fusion | bytes 12583296 | tf_op jit(solution)/shard_map/jit(_take)/gather | solution.py:75
  332.0 9.7 %fusion.17 = f32[96,64,512]{2,1,0:T(8,128)} fusion(bf16[96,512,64]{1,2,0:T(8,128)(2,1)} %gather_fusion.3, pred[96]{0:T(512)(128)(4,1)S(1)} %get-tuple-element.19, bf16[96,3,64,64]{3,2,0,1:T(8,128)(2,1)} %broadcast_select_fusion.4), kind=kOutput, calls=%fused_computation.38 | convolution fusion | flops 405798912 | bytes 20447328 | tf_op jit(solution)/shard_map/tkf,kdf->tkd/dot_general | solution.py:78
  341.7 0.0 copy-done
  341.7 11.0 %fusion = (bf16[512,96,64]{0,2,1:T(8,128)(2,1)}, f32[96,64,512]{2,1,0:T(8,128)}) fusion(f32[96,64,512]{2,1,0:T(8,128)} %fusion.17, bf16[96,512,64]{1,2,0:T(8,128)(2,1)S(1)} %copy-done, pred[96]{0:T(512)(128)(4,1)S(1)} %get-tuple-element.19, bf16[96,3,64,64]{3,2,0,1:T(8,128)(2,1)} %broadcast_select_fusion.4), kind=kOutput, calls=%fused_computation.7 | convolution fusion | flops 421527552 | bytes 39321696 | tf_op jit(solution)/shard_map/tkf,kdf->tkd/dot_general | solution.py:77
  352.7 9.6 %bitcast_convert_fusion = bf16[512,96,64]{0,2,1:T(8,128)(2,1)S(1)} fusion(f32[96,64,512]{2,1,0:T(8,128)} %get-tuple-element.18, f32[96,64,512]{2,1,0:T(8,128)} %fusion.17), kind=kLoop, calls=%fused_computation.6 | loop fusion | flops 6291456 | bytes 31457280 | tf_op jit(solution)/shard_map/convert_element_type | solution.py:16
  362.3 0.4 copy-done.1
  362.7 7.7 %fusion.32 = f32[64,512,64]{1,0,2:T(8,128)S(1)} fusion(bf16[512,96,64]{0,2,1:T(8,128)(2,1)S(1)} %copy-done.1, s32[96]{0:T(128)S(1)} %bitcast.191), kind=kOutput, calls=%fused_computation.53 | convolution fusion | flops 402659328 | bytes 14680448 | tf_op jit(solution)/shard_map/tkd,kr->trd/dot_general | solution.py:19
  370.5 5.0 %fusion.50 = bf16[512,64,64]{0,1,2:T(8,128)(2,1)S(1)} fusion(f32[64,512,64]{1,0,2:T(8,128)S(1)} %fusion.32, bf16[512,96,64]{0,2,1:T(8,128)(2,1)S(1)} %bitcast_convert_fusion, s32[96]{0:T(128)S(1)} %bitcast.192), kind=kOutput, calls=%fused_computation.77 | convolution fusion | flops 406853632 | bytes 18874752 | tf_op jit(solution)/shard_map/tkd,kr->trd/dot_general | solution.py:18
  375.5 4.4 copy.62
  379.9 6.7 %copy.69 = bf16[512,4096]{1,0:T(8,128)(2,1)} copy(bf16[512,4096]{0,1:T(8,128)(2,1)} %bitcast.183) | data formatting | bytes 8388608
  386.5 0.0 reduce-scatter.4.cloned.1.call-update
  386.6 5.2 %copy.63 = bf16[512,56,64]{0,2,1:T(8,128)(2,1)} copy(bf16[512,56,64]{0,1,2:T(8,128)(2,1)} %get-tuple-element.14) | data formatting | bytes 7340032 | tf_op jit(solution)/shard_map/convert_element_type | solution.py:69
  391.8 8.0 %gather_fusion.4 = bf16[96,512,64]{1,2,0:T(8,128)(2,1)} fusion(bf16[512,56,64]{0,2,1:T(8,128)(2,1)} %copy.63, s32[1024]{0:T(1024)S(1)} %pad_clamp_fusion), kind=kCustom, calls=%fused_computation.4.clone | custom fusion | bytes 12583296 | tf_op jit(solution)/shard_map/jit(_take)/gather | solution.py:76
  399.8 8.7 %fusion.55 = f32[96,1,64,64]{3,2,0,1:T(8,128)} fusion(bf16[96,512,64]{1,2,0:T(8,128)(2,1)} %gather_fusion.2, pred[96]{0:T(512)(128)(4,1)S(1)} %get-tuple-element.19, bf16[96,512,64]{1,2,0:T(8,128)(2,1)} %gather_fusion.1, pred[96]{0:T(512)(128)(4,1)S(1)} %get-tuple-element.20), kind=kOutput, calls=%fused_computation.81 | convolution fusion | flops 408944640 | bytes 14155968 | tf_op jit(solution)/shard_map/tkd,tkf->kdf/dot_general | solution.py:89
  408.5 8.6 %fusion.60 = f32[96,1,64,64]{3,2,0,1:T(8,128)} fusion(bf16[96,512,64]{1,2,0:T(8,128)(2,1)} %gather_fusion.3, pred[96]{0:T(512)(128)(4,1)S(1)} %get-tuple-element.19, bf16[96,512,64]{1,2,0:T(8,128)(2,1)} %gather_fusion.1, pred[96]{0:T(512)(128)(4,1)S(1)} %get-tuple-element.20), kind=kOutput, calls=%fused_computation.82 | convolution fusion | flops 408944640 | bytes 14155968 | tf_op jit(solution)/shard_map/tkd,tkf->kdf/dot_general | solution.py:90
  417.1 0.0 slice-done.2
  417.1 0.0 slice-done.4
  417.1 0.0 slice-done.3
  417.1 0.0 slice-done.5
  417.1 3.4 fusion.65
  420.5 9.7 %pad_maximum_fusion = f32[96,3,64,64]{3,2,0,1:T(8,128)} fusion(f32[96,1,64,64]{3,2,0,1:T(8,128)} %fusion.65, f32[96,1,64,64]{3,2,0,1:T(8,128)} %fusion.60, f32[96,1,64,64]{3,2,0,1:T(8,128)} %fusion.55), kind=kLoop, calls=%fused_computation.17 | loop fusion | flops 2359296 | bytes 9437184 | tf_op jit(solution)/shard_map/stack | solution.py:93
  430.2 9.6 %copy.64 = f32[96,3,64,64]{0,3,2,1:T(8,128)} copy(f32[96,3,64,64]{3,2,0,1:T(8,128)} %pad_maximum_fusion) | data formatting | bytes 9437184 | tf_op jit(solution)/shard_map/stack | solution.py:93
  439.8 3.0 multiply_convert_fusion
  442.9 2.6 copy.66
  445.5 1.5 copy.70
  447.0 1.7 fusion.70
  448.6 1.1 copy.65
  (19 shorter events, 0.1 us)
Async XLA Ops:
  7.2 60.7 %all-gather.3.cloned.1.call-start = ((), (), s32[]{:S(2)}) async-start(), calls=%async_computation.1 | async-start | bytes 4718592 | tf_op jit(solution)/shard_map/all_gather | solution.py:27
  9.3 178.1 %all-gather.5.cloned.1.call-start = ((), (), s32[]{:S(2)}) async-start(), calls=%async_computation.2 | async-start | bytes 4718592 | tf_op jit(solution)/shard_map/all_gather | solution.py:32
  10.0 435.4 %reduce-scatter.4.cloned.1.call-start = ((), (), s32[]{:S(2)}) async-start(), calls=%async_computation.3 | async-start | bytes 4718592
  10.7 10.8 %copy-start.4 = (s32[1,96]{1,0:T(1,128)S(1)}, s32[1,96]{1,0:T(1,128)}, u32[]{:S(2)}) copy-start(s32[1,96]{1,0:T(1,128)} %param.15) | copy-start | bytes 1156
  14.1 62.2 %copy-start.3 = (s32[1,96]{1,0:T(1,128)S(1)}, s32[1,96]{1,0:T(1,128)}, u32[]{:S(2)}) copy-start(s32[1,96]{1,0:T(1,128)} %param.16) | copy-start | bytes 1156
  74.4 176.4 %collective-permute-start = (bf16[1,512,4096]{1,2,0:T(8,128)(2,1)}, bf16[1,512,4096]{1,2,0:T(8,128)(2,1)}, u32[]{:S(2)}, u32[]{:S(2)}) collective-permute-start(bf16[1,512,4096]{1,2,0:T(8,128)(2,1)} %copy.46), channel_id=1, source_target_pairs={{8,0},{16,8},{24,16},{32,24},{40,32},{48,40},{56,48},{64,56},{72,6... | collective-permute-start | bytes 12582920 | tf_op jit(solution)/shard_map/ppermute | solution.py:12
  210.2 24.5 %slice-start = ((s8[6291456]{0:T(1024)(128)(4,1)}), s8[4194304]{0:T(1024)(128)(4,1)S(1)}, s32[]{:S(2)}) async-start(s8[6291456]{0:T(1024)(128)(4,1)} %bitcast.175), calls=%async_computation.4 | async-start | bytes 8388608
  223.7 11.0 %slice-start.1 = ((s8[6291456]{0:T(1024)(128)(4,1)}), s8[2097152]{0:T(1024)(128)(4,1)S(1)}, s32[]{:S(2)}) async-start(s8[6291456]{0:T(1024)(128)(4,1)} %bitcast.175), calls=%async_computation.5 | async-start | bytes 4194304
  307.5 5.2 %copy-start.2 = (bf16[512,56,64]{0,1,2:T(8,128)(2,1)S(1)}, bf16[512,56,64]{0,1,2:T(8,128)(2,1)}, u32[]{:S(2)}) copy-start(bf16[512,56,64]{0,1,2:T(8,128)(2,1)} %get-tuple-element.16) | copy-start | bytes 11010052
  332.0 9.7 %copy-start = (bf16[96,512,64]{1,2,0:T(8,128)(2,1)S(1)}, bf16[96,512,64]{1,2,0:T(8,128)(2,1)}, u32[]{:S(2)}) copy-start(bf16[96,512,64]{1,2,0:T(8,128)(2,1)} %gather_fusion.2) | copy-start | bytes 18874372
  352.7 10.0 %copy-start.1 = (bf16[512,96,64]{0,2,1:T(8,128)(2,1)S(1)}, bf16[512,96,64]{0,2,1:T(8,128)(2,1)}, u32[]{:S(2)}) copy-start(bf16[512,96,64]{0,2,1:T(8,128)(2,1)} %get-tuple-element.17) | copy-start | bytes 18874372
  399.8 17.3 %slice-start.2 = ((s8[6291456]{0:T(1024)(128)(4,1)}), s8[4194304]{0:T(1024)(128)(4,1)S(1)}, s32[]{:S(2)}) async-start(s8[6291456]{0:T(1024)(128)(4,1)} %bitcast.178), calls=%async_computation.6 | async-start | bytes 8388608
  399.8 17.3 %slice-start.4 = ((s8[6291456]{0:T(1024)(128)(4,1)}), s8[4194304]{0:T(1024)(128)(4,1)S(1)}, s32[]{:S(2)}) async-start(s8[6291456]{0:T(1024)(128)(4,1)} %bitcast.181), calls=%async_computation.8 | async-start | bytes 8388608
  408.5 8.6 %slice-start.3 = ((s8[6291456]{0:T(1024)(128)(4,1)}), s8[2097152]{0:T(1024)(128)(4,1)S(1)}, s32[]{:S(2)}) async-start(s8[6291456]{0:T(1024)(128)(4,1)} %bitcast.178), calls=%async_computation.7 | async-start | bytes 4194304
  408.5 8.6 %slice-start.5 = ((s8[6291456]{0:T(1024)(128)(4,1)}), s8[2097152]{0:T(1024)(128)(4,1)S(1)}, s32[]{:S(2)}) async-start(s8[6291456]{0:T(1024)(128)(4,1)} %bitcast.181), calls=%async_computation.9 | async-start | bytes 4194304
Sparse Core Ops, SparseCore 0:
  10.4 57.4 all-gather.2
  69.7 117.6 all-gather.4
  386.7 51.8 reduce-scatter.3
where the time goes:
time: 463 us; the launch traced here: 457 us
  waiting for transfers between devices  153 us (33%)
  matrix products  151 us (33%)
  local copies, waits for them, and re-layouts  105 us (23%)
  other arithmetic  30.9 us (7%)
  between operations  14.8 us (3%)
    all_gather x1, waiting for transfers between devices, per_device(): acts_all = lax.all_gather(acts, 'tensor', axis=1, tiled=True)  106 us
    dot_general x4, matrix products, spread(): jnp.einsum(form, high_part, hot_table, preferred_element_type=jnp.float32)  48.7 us
    all_gather x1, waiting for transfers between devices, per_device(): gathered = lax.all_gather(payload, 'tensor', axis=1, tiled=True)  46.3 us
    dot_general x4, matrix products, spread(): jnp.einsum(form, low_part, hot_table, preferred_element_type=jnp.float32)  42.3 us
    unnamed x27, local copies, waits for them, and re-layouts  15.7 us
    dot_general x1, matrix products, per_device(): jnp.einsum('tkf,kdf->tkd', g_slot, w_gate, preferred_element_type=jnp.flo...  11 us
    dot_general x1, matrix products, per_device(): jnp.einsum('tkf,kdf->tkd', u_slot, w_up, preferred_element_type=jnp.float32)  9.72 us
    another operation x1, other arithmetic, per_device(): jnp.stack([grad_gate, grad_up, grad_down], axis=1)  9.69 us
  transfers between devices with their start and end apart: 4, of which 2 were waited for; matrix products, arithmetic and copies ran while one was open for 32% of the time, Pallas kernels for 0%

commit v1 on v0

v1 whole, which is shorter than its diff:
```python
import functools

import jax
import jax.numpy as jnp
from jax import lax
from jax.experimental import pallas as pl
from jax.experimental.pallas import tpu as pltpu
from jax.sharding import PartitionSpec as P

MESH = pl.DeviceIdType.MESH
BF16 = jnp.bfloat16
F32 = jnp.float32

CAP = 96
ROWS = 64
WIDTH = 4096
TOK = 64
HALF = 256
SLOT = 12288
GROUP = 16
SPLIT = 1664

PARTS = (pl.ds(0, SPLIT), pl.ds(SPLIT, WIDTH - SPLIT))

ORD_C, ROW_C, KEEP_C = 0, 96, 192
ORD_R, POS_R, KEEP_R = 288, 384, 480
LAST_R, POS_K, ROW_K, ALIVE = 576, 640, 736, 832


def slot_order(keys):
    slots = jnp.arange(CAP, dtype=jnp.int32)
    same = keys[:, None] == keys[None, :]
    before = same & (slots[None, :] < slots[:, None])
    smaller = (keys[None, :] < keys[:, None]) | before
    rank = jnp.sum(smaller.astype(jnp.int32), axis=1)
    hot = (rank[None, :] == slots[:, None]).astype(jnp.int32)
    follows = jnp.max(before.astype(jnp.int32), axis=1)
    last = jnp.max(jnp.where(same, rank[None, :], 0), axis=1)
    return rank, hot, follows, last


def index_vector(row, col, live):
    slots = jnp.arange(CAP, dtype=jnp.int32)
    _, hot_c, follows_c, last_c = slot_order(col)
    rank_r, hot_r, follows_r, _ = slot_order(row)

    def in_order(hot, values):
        return jnp.sum(hot * values[None, :], axis=1)

    holds = row[None, :] == jnp.arange(ROWS, dtype=jnp.int32)[:, None]
    last_r = jnp.max(jnp.where(holds, rank_r[None, :] + 1, 0), axis=1)
    last_r = jnp.where(last_r == 0, CAP, last_r - 1)
    return jnp.concatenate(
        [
            in_order(hot_c, slots),
            in_order(hot_c, row),
            in_order(hot_c, follows_c),
            in_order(hot_r, slots),
            in_order(hot_r, last_c),
            in_order(hot_r, follows_r),
            last_r,
            last_c,
            row,
            slots < live,
        ]
    ).astype(jnp.int32)


def kernel(
    sections, index, acts, next_grad, head_grad, blocks, input_grad, block_grads,
    xc, dc, xt, dt, gu, hid, bk, wgu, wgut, wd, raw, part, rsa, rsb, rsz, zsum, s1, s2, acc, acc_b, ig,
    x_send, d_send, x_recv, d_recv, sh_send, a_send, a_recv, b_send, b_recv, z_send, z_recv, loc,
):
    s = lax.axis_index("section")
    t = lax.axis_index("tensor")
    y = lax.rem(t, 4)
    plane = t // 4

    def in_ring(step):
        return (s, plane * 4 + lax.rem(y + step, 4))

    across = (s, (1 - plane) * 4 + y)
    before = (lax.rem(s + sections - 1, sections), t)
    after = (lax.rem(s + 1, sections), t)

    barrier = pltpu.get_barrier_semaphore()
    for peer in (in_ring(1), in_ring(2), in_ring(3), across):
        pl.semaphore_signal(barrier, inc=1, device_id=peer, device_id_type=MESH)
    @pl.when(s < sections - 1)
    def _():
        pl.semaphore_signal(barrier, inc=1, device_id=after, device_id_type=MESH)

    blocks_in = pltpu.make_async_copy(blocks, raw, loc.at[0])
    blocks_in.start()
    own_in = pltpu.make_async_copy(acts, xc.at[0], loc.at[1])
    own_in.start()

    @pl.when(s > 0)
    def _():
        pl.semaphore_wait(barrier, 5)

    @pl.when(s == 0)
    def _():
        pl.semaphore_wait(barrier, 4)

    pending = []

    def send(src, dst, ssem, rsem, peer):
        copy = pltpu.make_async_remote_copy(
            src_ref=src, dst_ref=dst, send_sem=ssem, recv_sem=rsem, device_id=peer, device_id_type=MESH
        )
        copy.start()
        pending.append(copy)

    def arrived(dst, rsem):
        pltpu.make_async_remote_copy(
            src_ref=dst, dst_ref=dst, send_sem=rsem, recv_sem=rsem, device_id=across, device_id_type=MESH
        ).wait_recv()

    for p, cols in enumerate(PARTS):
        shift = pltpu.make_async_remote_copy(
            src_ref=next_grad.at[:, cols], dst_ref=dc.at[0, :, cols], send_sem=sh_send.at[p],
            recv_sem=d_recv.at[0, p], device_id=before, device_id_type=MESH,
        )

        @pl.when(s > 0)
        def _():
            shift.start()

        @pl.when(s == sections - 1)
        def _():
            pltpu.make_async_copy(head_grad.at[:, cols], dc.at[0, :, cols], d_recv.at[0, p]).start()

    def share_own(src, buf, ssem, rsem):
        for p, cols in enumerate(PARTS):
            send(src.at[:, cols], buf.at[4, :, cols], ssem.at[p], rsem.at[4, p], across)
            for step in (1, 3, 2):
                send(
                    src.at[:, cols], buf.at[4 - step, :, cols], ssem.at[2 * step + p], rsem.at[4 - step, p],
                    in_ring(step),
                )

    def pass_on_first(buf, ssem, rsem):
        cols = PARTS[0]
        arrived(buf.at[4, :, cols], rsem.at[4, 0])
        for step in (1, 3, 2):
            send(
                buf.at[4, :, cols], buf.at[8 - step, :, cols], ssem.at[7 + step], rsem.at[8 - step, 0], in_ring(step)
            )

    def pass_on_second(buf, ssem, rsem):
        cols = PARTS[1]
        for step in (1, 3, 2):
            arrived(buf.at[step, :, cols], rsem.at[step, 1])
            send(buf.at[step, :, cols], buf.at[4 + step, :, cols], ssem.at[10 + step], rsem.at[4 + step, 1], across)

    share_own(acts, xc, x_send, x_recv)

    blocks_in.wait()
    low = lax.broadcasted_iota(jnp.int32, (64, 128), 1) < 64
    low32 = lax.broadcasted_iota(jnp.int32, (32, 128), 1) < 64

    def prepare(g, _):
        rows = pl.ds(pl.multiple_of(g * GROUP, GROUP), GROUP)
        for i in range(SLOT // 128):
            s1[pl.ds(i * GROUP, GROUP), :] = raw[rows, pl.ds(i * 128, 128)].astype(F32)
        for j in range(GROUP):
            k = g * GROUP + j
            b = (j % 4) * 192
            for m in range(3):
                v = s1[pl.ds(m * 32 * GROUP + j, 32, stride=GROUP), :]
                turned = pltpu.roll(v, 64, 1)
                even, odd = (turned, v) if m == 1 else (v, turned)
                s2[pl.ds(b + m * 64, 32, stride=2), :] = even
                s2[pl.ds(b + m * 64 + 1, 32, stride=2), :] = odd
            both = jnp.where(low, s2[pl.ds(b, 64), :], s2[pl.ds(b + 64, 64), :])
            alive = index[ALIVE + k].astype(F32)
            both = both * alive
            down = s2[pl.ds(b + 128, 64), :] * alive
            wgu[k] = both.astype(BF16)
            wgut[k] = both.T.astype(BF16)
            wd[k] = down[:, :64].astype(BF16)
        return 0

    lax.fori_loop(0, CAP // GROUP, prepare, 0)
    bk[CAP] = jnp.zeros((64, HALF), BF16)

    for p, cols in enumerate(PARTS):
        arrived(dc.at[0, :, cols], d_recv.at[0, p])
    share_own(dc.at[0], dc, d_send, d_recv)
    pass_on_first(xc, x_send, x_recv)
    pass_on_first(dc, d_send, d_recv)
    pass_on_second(xc, x_send, x_recv)
    pass_on_second(dc, d_send, d_recv)

    def turn(buf, out, pair):
        def step(i, _):
            cols = pl.ds(pl.multiple_of(i * 128, 128), 128)
            tile = jnp.concatenate([buf[2 * pair, :, cols], buf[2 * pair + 1, :, cols]], axis=0)
            tile = tile.T
            out[2 * i, :, pl.ds(pair * 128, 128)] = tile[:64]
            out[2 * i + 1, :, pl.ds(pair * 128, 128)] = tile[64:]
            return 0

        lax.fori_loop(0, WIDTH // 128, step, 0, unroll=4)

    def forward(lanes):
        acc[...] = jnp.zeros_like(acc)

        def step(j, _):
            k, r = index[ORD_C + j], index[ROW_C + j]
            keep = index[KEEP_C + j].astype(F32)
            new = jnp.dot(wgut[k], xt[r, :, lanes], preferred_element_type=F32)
            hg = jnp.dot(wd[k], dt[r, :, lanes], preferred_element_type=F32)
            gate = new[:64] + keep * acc[pl.ds(0, 64), :]
            upper = new[64:] + keep * acc[pl.ds(64, 64), :]
            hg = hg + keep * acc[pl.ds(128, 64), :]
            acc[pl.ds(0, 64), :] = gate
            acc[pl.ds(64, 64), :] = upper
            acc[pl.ds(128, 64), :] = hg
            sg = jax.nn.sigmoid(gate)
            act = gate * sg
            hid[j, :, lanes] = (act * upper).astype(BF16)
            gu[j, pl.ds(0, 64), lanes] = (hg * upper * sg * (1.0 + gate * (1.0 - sg))).astype(BF16)
            gu[j, pl.ds(64, 64), lanes] = (hg * act).astype(BF16)
            return 0

        lax.fori_loop(0, CAP, step, 0, unroll=2)

    def backward(lanes, first_slot):
        acc_b[...] = jnp.zeros_like(acc_b)

        def step(j, _):
            k, p = index[ORD_R + j], index[POS_R + j]
            keep = index[KEEP_R + j].astype(F32)
            new = jnp.dot(wgu[k], gu[p, :, lanes], preferred_element_type=F32)
            new = new + keep * acc_b[...]
            acc_b[...] = new
            bk[j] = new.astype(BF16)
            return 0

        lax.fori_loop(0, CAP, step, 0, unroll=2)

        def place(i, _):
            cols = pl.ds(pl.multiple_of(i * 128, 128), 128)
            both = jnp.concatenate([bk[index[LAST_R + 2 * i]], bk[index[LAST_R + 2 * i + 1]]], axis=0)
            for q in range(2):
                tile = both[:, q * 128:(q + 1) * 128].T
                part[first_slot + 2 * q, :, cols] = tile[:64]
                part[first_slot + 2 * q + 1, :, cols] = tile[64:]
            return 0

        lax.fori_loop(0, ROWS // 2, place, 0, unroll=2)

    own_in.wait()
    for step in (1, 2, 3):
        arrived(xc.at[step, :, PARTS[0]], x_recv.at[step, 0])
    turn(xc, xt, 0)
    turn(xc, xt, 1)
    for step in (1, 2, 3):
        arrived(dc.at[step, :, PARTS[0]], d_recv.at[step, 0])
    turn(dc, dt, 0)
    turn(dc, dt, 1)
    forward(pl.ds(0, HALF))
    backward(pl.ds(0, HALF), 0)
    for step in (1, 3, 2):
        send(part.at[step], rsa.at[3 - step], a_send.at[step - 1], a_recv.at[3 - step], in_ring(step))

    def rest(buf, rsem):
        arrived(buf.at[4, :, PARTS[1]], rsem.at[4, 1])
        for step in (1, 2, 3):
            for p in range(2):
                arrived(buf.at[4 + step, :, PARTS[p]], rsem.at[4 + step, p])

    rest(xc, x_recv)
    turn(xc, xt, 2)
    turn(xc, xt, 3)
    rest(dc, d_recv)
    turn(dc, dt, 2)
    turn(dc, dt, 3)
    forward(pl.ds(HALF, HALF))
    backward(pl.ds(HALF, HALF), 4)
    for step in (1, 3, 2):
        send(part.at[4 + step], rsb.at[3 - step], b_send.at[step - 1], b_recv.at[3 - step], in_ring(step))

    def grads(g, _):
        for j in range(GROUP):
            k = g * GROUP + j
            p, r = index[POS_K + k], index[ROW_K + k]
            alive = index[ALIVE + k].astype(F32)
            turned = (((1,), (1,)), ((), ()))
            d_both = lax.dot_general(xt[r], gu[p], turned, preferred_element_type=F32)
            d_down = lax.dot_general(hid[p], dt[r], turned, preferred_element_type=F32)
            b = (j % 4) * 192
            s2[pl.ds(b, 64), :] = d_both * alive
            s2[pl.ds(b + 64, 64), pl.ds(0, 64)] = d_down * alive
            even, odd = s2[pl.ds(b, 32, stride=2), :], s2[pl.ds(b + 1, 32, stride=2), :]
            d_even, d_odd = s2[pl.ds(b + 64, 32, stride=2), :], s2[pl.ds(b + 65, 32, stride=2), :]
            s1[pl.ds(j, 32, stride=GROUP), :] = jnp.where(low32, even, pltpu.roll(odd, 64, 1))
            s1[pl.ds(32 * GROUP + j, 32, stride=GROUP), :] = jnp.where(low32, pltpu.roll(even, 64, 1), odd)
            s1[pl.ds(64 * GROUP + j, 32, stride=GROUP), :] = jnp.where(low32, d_even, pltpu.roll(d_odd, 64, 1))
        rows = pl.ds(pl.multiple_of(g * GROUP, GROUP), GROUP)
        for i in range(SLOT // 128):
            raw[rows, pl.ds(i * 128, 128)] = s1[pl.ds(i * GROUP, GROUP), :].astype(BF16)
        return 0

    lax.fori_loop(0, CAP // GROUP, grads, 0)
    blocks_out = pltpu.make_async_copy(raw, block_grads, loc.at[2])
    blocks_out.start()

    tiles = [(pl.ds(a, 16), pl.ds(b, 512)) for a in range(0, TOK, 16) for b in range(0, WIDTH, 512)]
    for n in range(3):
        arrived(rsb.at[n], b_recv.at[n])
    for rows, cols in tiles:
        total = part[4, rows, cols].astype(F32)
        for n in range(3):
            total = total + rsb[n, rows, cols].astype(F32)
        zsum[rows, cols] = total.astype(BF16)
    send(zsum, rsz, z_send, z_recv, across)
    for n in range(3):
        arrived(rsa.at[n], a_recv.at[n])
    arrived(rsz, z_recv)
    for rows, cols in tiles:
        total = part[0, rows, cols].astype(F32)
        for n in range(3):
            total = total + rsa[n, rows, cols].astype(F32)
        total = total + rsz[rows, cols].astype(F32)
        ig[rows, cols] = (dc[0, rows, cols].astype(F32) + total).astype(BF16)
    ig_out = pltpu.make_async_copy(ig, input_grad, loc.at[3])
    ig_out.start()

    for copy in pending:
        copy.wait_send()
    for p, cols in enumerate(PARTS):
        @pl.when(s > 0)
        def _():
            pltpu.make_async_remote_copy(
                src_ref=next_grad.at[:, cols], dst_ref=dc.at[0, :, cols], send_sem=sh_send.at[p],
                recv_sem=d_recv.at[0, p], device_id=before, device_id_type=MESH,
            ).wait_send()
    blocks_out.wait()
    ig_out.wait()


def per_device(sections, acts, next_grad, head_grad, blocks, block_row, block_col, live):
    index = index_vector(block_row[0], block_col[0], live[0])
    dma = pltpu.SemaphoreType.DMA
    any_space = pl.BlockSpec(memory_space=pl.ANY)
    input_grad, block_grads = pl.pallas_call(
        functools.partial(kernel, sections),
        out_shape=(
            jax.ShapeDtypeStruct((TOK, WIDTH), BF16),
            jax.ShapeDtypeStruct((CAP, SLOT), BF16),
        ),
        in_specs=[pl.BlockSpec(memory_space=pltpu.SMEM)] + [any_space] * 4,
        out_specs=(any_space, any_space),
        scratch_shapes=[
            pltpu.VMEM((8, TOK, WIDTH), BF16),
            pltpu.VMEM((8, TOK, WIDTH), BF16),
            pltpu.VMEM((ROWS, 64, 2 * HALF), BF16),
            pltpu.VMEM((ROWS, 64, 2 * HALF), BF16),
            pltpu.VMEM((CAP, 128, 2 * HALF), BF16),
            pltpu.VMEM((CAP, 64, 2 * HALF), BF16),
            pltpu.VMEM((CAP + 1, 64, HALF), BF16),
            pltpu.VMEM((CAP, 64, 128), BF16),
            pltpu.VMEM((CAP, 128, 64), BF16),
            pltpu.VMEM((CAP, 64, 64), BF16),
            pltpu.VMEM((CAP, SLOT), BF16),
            pltpu.VMEM((8, TOK, WIDTH), BF16),
            pltpu.VMEM((3, TOK, WIDTH), BF16),
            pltpu.VMEM((3, TOK, WIDTH), BF16),
            pltpu.VMEM((TOK, WIDTH), BF16),
            pltpu.VMEM((TOK, WIDTH), BF16),
            pltpu.VMEM((SLOT // 128 * GROUP, 128), F32),
            pltpu.VMEM((4 * 192, 128), F32),
            pltpu.VMEM((192, HALF), F32),
            pltpu.VMEM((64, HALF), F32),
            pltpu.VMEM((TOK, WIDTH), BF16),
            dma((14,)),
            dma((14,)),
            dma((8, 2)),
            dma((8, 2)),
            dma((2,)),
            dma((3,)),
            dma((3,)),
            dma((3,)),
            dma((3,)),
            dma,
            dma,
            dma((4,)),
        ],
        compiler_params=pltpu.CompilerParams(
            collective_id=0, has_side_effects=True, vmem_limit_bytes=63 * 2**20
        ),
    )(index, acts[0], next_grad[0], head_grad, blocks[0])
    return input_grad[None], block_grads[None]


def solution(mesh):
    return jax.shard_map(
        functools.partial(per_device, mesh.shape["section"]),
        mesh=mesh,
        in_specs=(
            P("section", "tensor", None),
            P("section", "tensor", None),
            P("tensor", None),
            P("section", "tensor", None),
            P("section", "tensor"),
            P("section", "tensor"),
            P("section", "tensor"),
        ),
        out_specs=(P("section", "tensor", None), P("section", "tensor", None)),
        check_vma=False,
    )
```

time: 463 us -> 148 us (0.32)
  waiting for transfers between devices: 153 us -> 0 us
  matrix products: 151 us -> 0 us
  Pallas kernels: 0 us -> 135 us
  local copies, waits for them, and re-layouts: 105 us -> 6.42 us
  other arithmetic: 30.9 us -> 2.87 us
  between operations: 14.8 us -> 1.32 us
    all_gather x2 -> x0, waiting for transfers between devices: 152 us -> none  [the longest x1 106 us: per_device(): acts_all = lax.all_gather(acts, 'tensor', axis=1, tiled=True)]
    dot_general x16 -> x0, matrix products: 151 us -> none  [the longest x4 48.7 us: spread(): jnp.einsum(form, high_part, hot_table, preferred_element_type=jnp.float32)]
    pallas_call x0 -> x1, Pallas kernels: none -> 135 us  [per_device(): pl.pallas_call(functools.partial(kernel, sections), out_shape=(jax.ShapeD...]
    gather x5 -> x0, local copies, waits for them, and re-layouts: 40.9 us -> none  [the longest x1 8.38 us: per_device(): x_slot = jnp.take(act_blocks, row_ids, axis=1)]
    convert_element_type x4 -> x0, local copies, waits for them, and re-layouts: 17.9 us -> none  [the longest x1 5.23 us: per_device(): hidden = (activated * upper).astype(jnp.bfloat16)]
    all_gather x2 -> x0, local copies, waits for them, and re-layouts: 13.1 us -> none  [the longest x1 6.6 us: per_device(): acts_all = lax.all_gather(acts, 'tensor', axis=1, tiled=True)]
    convert_element_type x3 -> x1, other arithmetic: 12.6 us -> 0.01 us  [index_vector(): jnp.concatenate([in_order(hot_c, slots), in_order(hot_c, row), in_order(h...]
    unnamed x27 -> x2, local copies, waits for them, and re-layouts: 15.7 us -> 5.09 us
  transfers between devices with their start and end apart: 4 -> 0, of which waited for: 2 -> 0; matrix products, arithmetic and copies ran while one was open for 32% -> 0% of each run, Pallas kernels for 0% -> 0%
where the time goes in v1:
time: 148 us; the launch traced here: 145 us
  Pallas kernels  135 us (91%)
  local copies, waits for them, and re-layouts  6.42 us (4%)
  other arithmetic  2.87 us (2%)
    pallas_call x1, Pallas kernels, per_device(): pl.pallas_call(functools.partial(kernel, sections), out_shape=(jax.ShapeD...  135 us
    unnamed x2, local copies, waits for them, and re-layouts  5.09 us

profile of v1, /device:TPU:64, one launch (start us, length us, event | category | flops | bytes accessed | tf_op | source)
XLA Modules:
  0.0 145.3 jit_solution(6069941157675854469)
XLA Ops:
  1.3 0.9 convert_reduce_fusion.3
  2.2 1.0 convert_reduce_fusion
  3.2 0.8 select_reduce_fusion.6
  4.0 0.1 select_reduce_fusion
  4.2 1.3 concatenate.3.index
  5.5 134.7 %shard_map.86 = (bf16[64,4096]{1,0:T(8,128)(2,1)}, bf16[96,12288]{1,0:T(8,128)(2,1)}) custom-call(s32[928]{0:T(1024)} %concatenate.3.index, bf16[64,4096]{1,0:T(8,128)(2,1)} %bitcast.11, bf16[64,4096]{1,0:T(8,128)(2,1)} %bitcast.12, bf16[64,4096]{1,0:T(8,128)(2,1)} %head_grad.1, bf16[96,12288]{1,0:T(8,128)(2,1)} %bitcast.9), custom_call_target="tpu_custom_call" | custom-call | tf_op jit(solution)/shard_map/pallas_call | solution.py:349
  140.2 1.9 %copy.12 = bf16[1,64,4096]{2,1,0:T(8,128)(2,1)} copy(bf16[1,64,4096]{2,1,0:T(8,128)(2,1)} %bitcast.13) | data formatting | bytes 1048576
  142.1 3.2 %copy.13 = bf16[1,96,12288]{2,1,0:T(8,128)(2,1)} copy(bf16[1,96,12288]{2,1,0:T(8,128)(2,1)} %bitcast.10) | data formatting | bytes 4718592
  (3 shorter events, 0.0 us)

commit v2 on v1

v2 whole, which is shorter than its diff:
```python
import functools

import jax
import jax.numpy as jnp
from jax import lax
from jax.experimental import pallas as pl
from jax.experimental.pallas import tpu as pltpu
from jax.sharding import PartitionSpec as P

MESH = pl.DeviceIdType.MESH
BF16 = jnp.bfloat16
F32 = jnp.float32

CAP = 96
ROWS = 64
WIDTH = 4096
TOK = 64
HALF = 256
SLOT = 12288
GROUP = 16
SPLIT = 2048
REST = WIDTH - SPLIT

PARTS = (pl.ds(0, SPLIT), pl.ds(SPLIT, REST))
HALVES = (
    (pl.ds(0, SPLIT // 2), pl.ds(SPLIT // 2, SPLIT // 2)),
    (pl.ds(SPLIT, REST // 2), pl.ds(SPLIT + REST // 2, REST // 2)),
)

ORD_C, ROW_C, KEEP_C, ORD_R, POS_R, KEEP_R, LAST_R, POS_K, ROW_K, ALIVE = range(10)
QUARTERS = tuple(pl.ds(n * WIDTH // 4, WIDTH // 4) for n in range(4))


def fill_table(live_ref, row_ref, col_ref, table):
    table[...] = jnp.zeros_like(table)
    lane = lax.broadcasted_iota(jnp.int32, (CAP, CAP), 1).astype(F32)
    sub = lax.broadcasted_iota(jnp.int32, (CAP, CAP), 0).astype(F32)
    one, none = jnp.ones((CAP, CAP), F32), jnp.zeros((CAP, CAP), F32)

    def both_ways(ref):
        along = jnp.broadcast_to(ref[...].astype(F32), (CAP, CAP))
        down = jnp.sum(jnp.where(lane == sub, along, none), axis=1, keepdims=True)
        return along, jnp.broadcast_to(down, (CAP, CAP))

    def sort(along, down):
        same = along == down
        ahead = jnp.where(same & (lane < sub), one, none)
        behind = jnp.where(same & (sub < lane), one, none)
        rank_down = jnp.sum(jnp.where(along < down, one, ahead), axis=1, keepdims=True)
        rank_along = jnp.sum(jnp.where(down < along, one, behind), axis=0, keepdims=True)
        follows = jnp.max(ahead, axis=1, keepdims=True)
        wide = jnp.broadcast_to(rank_down, (CAP, CAP))
        last_along = jnp.max(jnp.where(same, wide, none), axis=0, keepdims=True)
        last_down = jnp.max(
            jnp.where(same, jnp.broadcast_to(rank_along, (CAP, CAP)), none), axis=1, keepdims=True
        )
        return wide, jnp.broadcast_to(follows, (CAP, CAP)), last_along, jnp.broadcast_to(last_down, (CAP, CAP))

    row_along, row_down = both_ways(row_ref)
    col_along, col_down = both_ways(col_ref)
    rank_c, follows_c, last_along, last_down = sort(col_along, col_down)
    rank_r, follows_r, _, _ = sort(row_along, row_down)

    def put(place, values):
        table[pl.ds(place, 1), pl.ds(0, CAP)] = values.astype(jnp.int32)

    def in_order(rank, values):
        return jnp.sum(jnp.where(rank == lane, values, none), axis=0, keepdims=True)

    put(ORD_C, in_order(rank_c, sub))
    put(ROW_C, in_order(rank_c, row_down))
    put(KEEP_C, in_order(rank_c, follows_c))
    put(ORD_R, in_order(rank_r, sub))
    put(POS_R, in_order(rank_r, last_down))
    put(KEEP_R, in_order(rank_r, follows_r))
    ends = jnp.max(jnp.where(row_down == lane, rank_r + 1.0, none), axis=0, keepdims=True)
    put(LAST_R, jnp.where(ends == 0.0, jnp.full((1, CAP), CAP, F32), ends - 1.0))
    put(POS_K, last_along)
    put(ROW_K, row_along[:1])
    put(ALIVE, jnp.where(lane[:1] < live_ref[0, 0].astype(F32), one[:1], none[:1]))


def kernel(
    sections, index, acts, next_grad, head_grad, blocks, input_grad, block_grads,
    xc, dc, xt, dt, gu, hid, bk, wgu, wf, raw, part, hop_a, hop_b, rec_a, rec_b, rsz,
    zsum, s1, s2, acc, acc_b, ig,
    x_send, d_send, x_recv, d_recv, sh_send, ra_send, ra_hop, ra_recv, rb_send, rb_hop, rb_recv, z_send, z_recv, loc,
):
    s = lax.axis_index("section")
    t = lax.axis_index("tensor")
    y = lax.rem(t, 4)
    plane = t // 4

    def in_ring(step):
        return (s, plane * 4 + lax.rem(y + step, 4))

    across = (s, (1 - plane) * 4 + y)
    before = (lax.rem(s + sections - 1, sections), t)
    after = (lax.rem(s + 1, sections), t)

    barrier = pltpu.get_barrier_semaphore()
    for peer in (in_ring(1), in_ring(2), in_ring(3), across):
        pl.semaphore_signal(barrier, inc=1, device_id=peer, device_id_type=MESH)
    @pl.when(s < sections - 1)
    def _():
        pl.semaphore_signal(barrier, inc=1, device_id=after, device_id_type=MESH)

    blocks_in = pltpu.make_async_copy(blocks, raw, loc.at[0])
    blocks_in.start()
    own_in = pltpu.make_async_copy(acts, xc.at[0], loc.at[1])
    own_in.start()

    @pl.when(s > 0)
    def _():
        pl.semaphore_wait(barrier, 5)

    @pl.when(s == 0)
    def _():
        pl.semaphore_wait(barrier, 4)

    pending = []

    def send(src, dst, ssem, rsem, peer):
        copy = pltpu.make_async_remote_copy(
            src_ref=src, dst_ref=dst, send_sem=ssem, recv_sem=rsem, device_id=peer, device_id_type=MESH
        )
        copy.start()
        pending.append(copy)

    def arrived(dst, rsem):
        pltpu.make_async_remote_copy(
            src_ref=dst, dst_ref=dst, send_sem=rsem, recv_sem=rsem, device_id=across, device_id_type=MESH
        ).wait_recv()

    for p, cols in enumerate(PARTS):
        shift = pltpu.make_async_remote_copy(
            src_ref=next_grad.at[:, cols], dst_ref=dc.at[0, :, cols], send_sem=sh_send.at[p],
            recv_sem=d_recv.at[0, 2 * p], device_id=before, device_id_type=MESH,
        )

        @pl.when(s > 0)
        def _():
            shift.start()

        @pl.when(s == sections - 1)
        def _():
            pltpu.make_async_copy(head_grad.at[:, cols], dc.at[0, :, cols], d_recv.at[0, 2 * p]).start()

    def share_own(src, buf, ssem, rsem):
        for p, cols in enumerate(PARTS):
            send(src.at[:, cols], buf.at[4, :, cols], ssem.at[p], rsem.at[4, 2 * p], across)
            for step in (1, 3):
                send(
                    src.at[:, cols], buf.at[4 - step, :, cols], ssem.at[step + 1 + p], rsem.at[4 - step, 2 * p],
                    in_ring(step),
                )

    def round_own(buf, ssem, rsem):
        for p in (1, 0):
            for way, (place, step) in enumerate(((3, 1), (1, 3))):
                arrived(buf.at[place, :, PARTS[p]], rsem.at[place, 2 * p])
                cols = HALVES[p][way]
                send(
                    buf.at[place, :, cols], buf.at[2, :, cols], ssem.at[6 + 2 * p + way], rsem.at[2, 2 * p + way],
                    in_ring(step),
                )
        for place in (1, 3):
            cols = PARTS[1]
            send(
                buf.at[place, :, cols], buf.at[4 + place, :, cols], ssem.at[10 + place // 2], rsem.at[4 + place, 2],
                across,
            )

    def share_first(buf, ssem, rsem):
        cols = PARTS[0]
        arrived(buf.at[4, :, cols], rsem.at[4, 0])
        for step in (1, 3):
            send(
                buf.at[4, :, cols], buf.at[8 - step, :, cols], ssem.at[12 + step // 2], rsem.at[8 - step, 0],
                in_ring(step),
            )

    def cross_last(buf, ssem, rsem):
        for p in range(2):
            for way in range(2):
                arrived(buf.at[2, :, HALVES[p][way]], rsem.at[2, 2 * p + way])
        send(buf.at[2, :, PARTS[1]], buf.at[6, :, PARTS[1]], ssem.at[14], rsem.at[6, 2], across)

    def round_first(buf, ssem, rsem):
        for way, (place, step) in enumerate(((7, 1), (5, 3))):
            arrived(buf.at[place, :, PARTS[0]], rsem.at[place, 0])
            cols = HALVES[0][way]
            send(buf.at[place, :, cols], buf.at[6, :, cols], ssem.at[15 + way], rsem.at[6, way], in_ring(step))

    def rest(buf, rsem):
        for place in (4, 5, 7, 6):
            arrived(buf.at[place, :, PARTS[1]], rsem.at[place, 2])
        for way in range(2):
            arrived(buf.at[6, :, HALVES[0][way]], rsem.at[6, way])

    share_own(acts, xc, x_send, x_recv)

    blocks_in.wait()
    low = lax.broadcasted_iota(jnp.int32, (64, 128), 1) < 64
    low32 = lax.broadcasted_iota(jnp.int32, (32, 128), 1) < 64

    def prepare(g, _):
        rows = pl.ds(pl.multiple_of(g * GROUP, GROUP), GROUP)
        for i in range(SLOT // 128):
            s1[pl.ds(i * GROUP, GROUP), :] = raw[rows, pl.ds(i * 128, 128)].astype(F32)
        for j in range(GROUP):
            k = g * GROUP + j
            b = (j % 4) * 192
            for m in range(3):
                v = s1[pl.ds(m * 32 * GROUP + j, 32, stride=GROUP), :]
                turned = pltpu.roll(v, 64, 1)
                even, odd = (turned, v) if m == 1 else (v, turned)
                s2[pl.ds(b + m * 64, 32, stride=2), :] = even
                s2[pl.ds(b + m * 64 + 1, 32, stride=2), :] = odd
            both = jnp.where(low, s2[pl.ds(b, 64), :], s2[pl.ds(b + 64, 64), :])
            alive = index[ALIVE, k].astype(F32)
            both = both * alive
            down = s2[pl.ds(b + 128, 64), :] * alive
            wgu[k] = both.astype(BF16)
            wf[k, pl.ds(0, 128), pl.ds(0, 64)] = both.T.astype(BF16)
            wf[k, pl.ds(0, 128), pl.ds(64, 64)] = jnp.zeros((128, 64), BF16)
            wf[k, pl.ds(128, 64), :] = jnp.where(low, 0.0, pltpu.roll(down, 64, 1)).astype(BF16)
        return 0

    lax.fori_loop(0, CAP // GROUP // 2, prepare, 0)

    for p, cols in enumerate(PARTS):
        arrived(dc.at[0, :, cols], d_recv.at[0, 2 * p])
    share_own(dc.at[0], dc, d_send, d_recv)
    lax.fori_loop(CAP // GROUP // 2, CAP // GROUP, prepare, 0)
    bk[CAP] = jnp.zeros((64, HALF), BF16)

    def turn(buf, out, pair):
        def step(i, _):
            cols = pl.ds(pl.multiple_of(i * 128, 128), 128)
            tile = jnp.concatenate([buf[2 * pair, :, cols], buf[2 * pair + 1, :, cols]], axis=0)
            tile = tile.T
            out[2 * i, :, pl.ds(pair * 128, 128)] = tile[:64]
            out[2 * i + 1, :, pl.ds(pair * 128, 128)] = tile[64:]
            return 0

        lax.fori_loop(0, WIDTH // 128, step, 0, unroll=4)

    def forward(lanes):
        acc[...] = jnp.zeros_like(acc)

        def step(i, _):
            slots = [2 * i, 2 * i + 1]
            tokens, weights = [], []
            for j in slots:
                r = index[ROW_C, j]
                tokens += [xt[r, :, lanes], dt[r, :, lanes]]
                weights.append(wf[index[ORD_C, j]])
            none = jnp.zeros((192, 128), BF16)
            weights = jnp.concatenate(
                [jnp.concatenate([weights[0], none], axis=1), jnp.concatenate([none, weights[1]], axis=1)], axis=0
            )
            new = jnp.dot(weights, jnp.concatenate(tokens, axis=0), preferred_element_type=F32)
            total = acc[...]
            for n, j in enumerate(slots):
                total = new[n * 192:(n + 1) * 192] + index[KEEP_C, j].astype(F32) * total
                gate, upper, hg = total[:64], total[64:128], total[128:]
                sg = 0.5 + 0.5 * jnp.tanh(0.5 * gate)
                act = gate * sg
                hid[j, :, lanes] = (act * upper).astype(BF16)
                gu[j, pl.ds(0, 64), lanes] = (hg * upper * sg * (1.0 + gate * (1.0 - sg))).astype(BF16)
                gu[j, pl.ds(64, 64), lanes] = (hg * act).astype(BF16)
            acc[...] = total
            return 0

        lax.fori_loop(0, CAP // 2, step, 0, unroll=4)

    def backward(lanes, first_slot):
        acc_b[...] = jnp.zeros_like(acc_b)

        def step(i, _):
            slots = [2 * i, 2 * i + 1]
            none = jnp.zeros((64, 128), BF16)
            first, second = (wgu[index[ORD_R, j]] for j in slots)
            weights = jnp.concatenate(
                [jnp.concatenate([first, none], axis=1), jnp.concatenate([none, second], axis=1)], axis=0
            )
            both = jnp.concatenate([gu[index[POS_R, j], :, lanes] for j in slots], axis=0)
            new = jnp.dot(weights, both, preferred_element_type=F32)
            total = acc_b[...]
            for n, j in enumerate(slots):
                total = new[n * 64:(n + 1) * 64] + index[KEEP_R, j].astype(F32) * total
                bk[j] = total.astype(BF16)
            acc_b[...] = total
            return 0

        lax.fori_loop(0, CAP // 2, step, 0, unroll=4)

        def place(i, _):
            cols = pl.ds(pl.multiple_of(i * 128, 128), 128)
            both = jnp.concatenate([bk[index[LAST_R, 2 * i]], bk[index[LAST_R, 2 * i + 1]]], axis=0)
            for q in range(2):
                tile = both[:, q * 128:(q + 1) * 128].T
                part[first_slot + 2 * q, :, cols] = tile[:64]
                part[first_slot + 2 * q + 1, :, cols] = tile[64:]
            return 0

        lax.fori_loop(0, ROWS // 2, place, 0, unroll=2)

    def start_round(base, hop, rec, ssem, hsem, rsem):
        for n in range(2):
            here = pl.ds(n * WIDTH // 4, WIDTH // 4)
            up, down = QUARTERS[n], QUARTERS[2 + n]
            send(part.at[base + 2, :, up], hop.at[0, :, here], ssem.at[0, n], hsem.at[0, n], in_ring(1))
            send(part.at[base + 2, :, down], hop.at[1, :, here], ssem.at[1, n], hsem.at[1, n], in_ring(3))
            send(part.at[base + 1, :, down], rec.at[0, :, down], ssem.at[2, n], rsem.at[0, 2 + n], in_ring(1))
            send(part.at[base + 3, :, up], rec.at[1, :, up], ssem.at[3, n], rsem.at[1, n], in_ring(3))

    def add_round(base, n, hop, rec, ssem, hsem, rsem):
        here = pl.ds(n * WIDTH // 4, WIDTH // 4)
        for way, (place, step, q) in enumerate(((1, 1, n), (3, 3, 2 + n))):
            cols = QUARTERS[q]
            arrived(hop.at[way, :, here], hsem.at[way, n])
            part[base + place, :, cols] = (
                part[base + place, :, cols].astype(F32) + hop[way, :, here].astype(F32)
            ).astype(BF16)
            send(part.at[base + place, :, cols], rec.at[way, :, cols], ssem.at[4 + way, n], rsem.at[way, q], in_ring(step))

    own_in.wait()
    round_own(xc, x_send, x_recv)
    share_first(xc, x_send, x_recv)
    turn(xc, xt, 0)
    round_own(dc, d_send, d_recv)
    share_first(dc, d_send, d_recv)
    turn(dc, dt, 0)
    cross_last(xc, x_send, x_recv)
    turn(xc, xt, 1)
    cross_last(dc, d_send, d_recv)
    turn(dc, dt, 1)
    forward(pl.ds(0, HALF))
    round_first(xc, x_send, x_recv)
    round_first(dc, d_send, d_recv)
    backward(pl.ds(0, HALF), 0)
    start_round(0, hop_a, rec_a, ra_send, ra_hop, ra_recv)

    rest(xc, x_recv)
    turn(xc, xt, 2)
    turn(xc, xt, 3)
    add_round(0, 0, hop_a, rec_a, ra_send, ra_hop, ra_recv)
    rest(dc, d_recv)
    turn(dc, dt, 2)
    add_round(0, 1, hop_a, rec_a, ra_send, ra_hop, ra_recv)
    turn(dc, dt, 3)
    forward(pl.ds(HALF, HALF))
    backward(pl.ds(HALF, HALF), 4)
    start_round(4, hop_b, rec_b, rb_send, rb_hop, rb_recv)

    def grads(g, _):
        for j in range(GROUP):
            k = g * GROUP + j
            p, r = index[POS_K, k], index[ROW_K, k]
            alive = index[ALIVE, k].astype(F32)
            turned = (((1,), (1,)), ((), ()))
            d_both = lax.dot_general(xt[r], gu[p], turned, preferred_element_type=F32)
            d_down = lax.dot_general(hid[p], dt[r], turned, preferred_element_type=F32)
            b = (j % 4) * 192
            s2[pl.ds(b, 64), :] = d_both * alive
            s2[pl.ds(b + 64, 64), pl.ds(0, 64)] = d_down * alive
            even, odd = s2[pl.ds(b, 32, stride=2), :], s2[pl.ds(b + 1, 32, stride=2), :]
            d_even, d_odd = s2[pl.ds(b + 64, 32, stride=2), :], s2[pl.ds(b + 65, 32, stride=2), :]
            s1[pl.ds(j, 32, stride=GROUP), :] = jnp.where(low32, even, pltpu.roll(odd, 64, 1))
            s1[pl.ds(32 * GROUP + j, 32, stride=GROUP), :] = jnp.where(low32, pltpu.roll(even, 64, 1), odd)
            s1[pl.ds(64 * GROUP + j, 32, stride=GROUP), :] = jnp.where(low32, d_even, pltpu.roll(d_odd, 64, 1))
        rows = pl.ds(pl.multiple_of(g * GROUP, GROUP), GROUP)
        for i in range(SLOT // 128):
            raw[rows, pl.ds(i * 128, 128)] = s1[pl.ds(i * GROUP, GROUP), :].astype(BF16)
        return 0

    lax.fori_loop(0, 2, grads, 0)
    add_round(4, 0, hop_b, rec_b, rb_send, rb_hop, rb_recv)
    lax.fori_loop(2, 4, grads, 0)
    add_round(4, 1, hop_b, rec_b, rb_send, rb_hop, rb_recv)
    lax.fori_loop(4, CAP // GROUP, grads, 0)
    blocks_out = pltpu.make_async_copy(raw, block_grads, loc.at[2])
    blocks_out.start()

    for q in (0, 2, 1, 3):
        cols = QUARTERS[q]
        for n in range(2):
            arrived(rec_b.at[n, :, cols], rb_recv.at[n, q])
        zsum[:, cols] = (
            part[4, :, cols].astype(F32) + rec_b[0, :, cols].astype(F32) + rec_b[1, :, cols].astype(F32)
        ).astype(BF16)
        send(zsum.at[:, cols], rsz.at[:, cols], z_send.at[q], z_recv.at[q], across)
    outs = []
    for q in (0, 2, 1, 3):
        cols = QUARTERS[q]
        for n in range(2):
            arrived(rec_a.at[n, :, cols], ra_recv.at[n, q])
        total = part[0, :, cols].astype(F32) + rec_a[0, :, cols].astype(F32) + rec_a[1, :, cols].astype(F32)
        arrived(rsz.at[:, cols], z_recv.at[q])
        total = total + rsz[:, cols].astype(F32)
        ig[:, cols] = (dc[0, :, cols].astype(F32) + total).astype(BF16)
        copy = pltpu.make_async_copy(ig.at[:, cols], input_grad.at[:, cols], loc.at[3 + q])
        copy.start()
        outs.append(copy)

    for copy in pending:
        copy.wait_send()
    for p, cols in enumerate(PARTS):
        @pl.when(s > 0)
        def _():
            pltpu.make_async_remote_copy(
                src_ref=next_grad.at[:, cols], dst_ref=dc.at[0, :, cols], send_sem=sh_send.at[p],
                recv_sem=d_recv.at[0, 2 * p], device_id=before, device_id_type=MESH,
            ).wait_send()
    blocks_out.wait()
    for copy in outs:
        copy.wait()


def per_device(sections, acts, next_grad, head_grad, blocks, block_row, block_col, live):
    index = pl.pallas_call(
        fill_table,
        out_shape=jax.ShapeDtypeStruct((16, 128), jnp.int32),
        in_specs=[pl.BlockSpec(memory_space=pltpu.SMEM)] + [pl.BlockSpec(memory_space=pltpu.VMEM)] * 2,
        out_specs=pl.BlockSpec(memory_space=pltpu.VMEM),
    )(live, block_row, block_col)
    dma = pltpu.SemaphoreType.DMA
    any_space = pl.BlockSpec(memory_space=pl.ANY)
    input_grad, block_grads = pl.pallas_call(
        functools.partial(kernel, sections),
        out_shape=(
            jax.ShapeDtypeStruct((TOK, WIDTH), BF16),
            jax.ShapeDtypeStruct((CAP, SLOT), BF16),
        ),
        in_specs=[pl.BlockSpec(memory_space=pltpu.SMEM)] + [any_space] * 4,
        out_specs=(any_space, any_space),
        scratch_shapes=[
            pltpu.VMEM((8, TOK, WIDTH), BF16),
            pltpu.VMEM((8, TOK, WIDTH), BF16),
            pltpu.VMEM((ROWS, 64, 2 * HALF), BF16),
            pltpu.VMEM((ROWS, 64, 2 * HALF), BF16),
            pltpu.VMEM((CAP, 128, 2 * HALF), BF16),
            pltpu.VMEM((CAP, 64, 2 * HALF), BF16),
            pltpu.VMEM((CAP + 1, 64, HALF), BF16),
            pltpu.VMEM((CAP, 64, 128), BF16),
            pltpu.VMEM((CAP, 192, 128), BF16),
            pltpu.VMEM((CAP, SLOT), BF16),
            pltpu.VMEM((8, TOK, WIDTH), BF16),
            pltpu.VMEM((2, TOK, WIDTH // 2), BF16),
            pltpu.VMEM((2, TOK, WIDTH // 2), BF16),
            pltpu.VMEM((2, TOK, WIDTH), BF16),
            pltpu.VMEM((2, TOK, WIDTH), BF16),
            pltpu.VMEM((TOK, WIDTH), BF16),
            pltpu.VMEM((TOK, WIDTH), BF16),
            pltpu.VMEM((SLOT // 128 * GROUP, 128), F32),
            pltpu.VMEM((4 * 192, 128), F32),
            pltpu.VMEM((192, HALF), F32),
            pltpu.VMEM((64, HALF), F32),
            pltpu.VMEM((TOK, WIDTH), BF16),
            dma((17,)),
            dma((17,)),
            dma((8, 4)),
            dma((8, 4)),
            dma((2,)),
            dma((6, 2)),
            dma((2, 2)),
            dma((2, 4)),
            dma((6, 2)),
            dma((2, 2)),
            dma((2, 4)),
            dma((4,)),
            dma((4,)),
            dma((7,)),
        ],
        compiler_params=pltpu.CompilerParams(
            collective_id=0, has_side_effects=True, vmem_limit_bytes=63 * 2**20
        ),
    )(index, acts[0], next_grad[0], head_grad, blocks[0])
    return input_grad[None], block_grads[None]


def solution(mesh):
    return jax.shard_map(
        functools.partial(per_device, mesh.shape["section"]),
        mesh=mesh,
        in_specs=(
            P("section", "tensor", None),
            P("section", "tensor", None),
            P("tensor", None),
            P("section", "tensor", None),
            P("section", "tensor"),
            P("section", "tensor"),
            P("section", "tensor"),
        ),
        out_specs=(P("section", "tensor", None), P("section", "tensor", None)),
        check_vma=False,
    )
```

time: 148 us -> 118 us (0.80)
  the two profiles are of different devices: /device:TPU:64 before, /device:TPU:39 now
where the time goes in v2:
time: 118 us
  Pallas kernels  112 us (95%)
  local copies, waits for them, and re-layouts  5.09 us (4%)
  between operations  1.29 us (1%)
    pallas_call x1, Pallas kernels, per_device(): pl.pallas_call(functools.partial(kernel, sections), out_shape=(jax.ShapeD...  110 us
    unnamed x2, local copies, waits for them, and re-layouts  5.09 us

profile of v2, /device:TPU:39, one launch (start us, length us, event | category | flops | bytes accessed | tf_op | source)
XLA Modules:
  0.0 118.2 jit_solution(5335013911615638799)
XLA Ops:
  1.3 1.5 %shard_map.86.index = s32[16,128]{1,0:T(8,128)} custom-call(s32[1,1]{1,0:T(1,128)S(6)} %copy.11.live_ref, s32[1,96]{1,0:T(1,128)} %row_ref.1, s32[1,96]{1,0:T(1,128)} %col_ref.1), custom_call_target="tpu_custom_call" | custom-call | tf_op jit(solution)/shard_map/pallas_call | solution.py:423
  2.8 110.3 %shard_map.87 = (bf16[64,4096]{1,0:T(8,128)(2,1)}, bf16[96,12288]{1,0:T(8,128)(2,1)}) custom-call(s32[16,128]{1,0:T(8,128)} %shard_map.86.index, bf16[64,4096]{1,0:T(8,128)(2,1)} %bitcast.7, bf16[64,4096]{1,0:T(8,128)(2,1)} %bitcast.8, bf16[64,4096]{1,0:T(8,128)(2,1)} %head_grad.1, bf16[96,12288]{1,0:T(8,128)(2,1)} %bitcast.6), custom_call_target="tpu_custom_call" | custom-call | tf_op jit(solution)/shard_map/pallas_call | solution.py:431
  113.1 1.9 %copy.12 = bf16[1,64,4096]{2,1,0:T(8,128)(2,1)} copy(bf16[1,64,4096]{2,1,0:T(8,128)(2,1)} %bitcast.9) | data formatting | bytes 1048576
  115.0 3.2 %copy.13 = bf16[1,96,12288]{2,1,0:T(8,128)(2,1)} copy(bf16[1,96,12288]{2,1,0:T(8,128)(2,1)} %bitcast.5) | data formatting | bytes 4718592

commit v3 on v2

--- a/solution.py
+++ b/solution.py
@@ -28,7 +28,7 @@
 )
 
 ORD_C, ROW_C, KEEP_C, ORD_R, POS_R, KEEP_R, LAST_R, POS_K, ROW_K, ALIVE = range(10)
-QUARTERS = tuple(pl.ds(n * WIDTH // 4, WIDTH // 4) for n in range(4))
+PIECES_A, PIECES_B = 2, 4
 
 
 def fill_table(live_ref, row_ref, col_ref, table):
@@ -192,8 +192,12 @@
             cols = HALVES[0][way]
             send(buf.at[place, :, cols], buf.at[6, :, cols], ssem.at[15 + way], rsem.at[6, way], in_ring(step))
 
-    def rest(buf, rsem):
-        for place in (4, 5, 7, 6):
+    def rest_near(buf, rsem):
+        for place in (5, 7):
+            arrived(buf.at[place, :, PARTS[1]], rsem.at[place, 2])
+
+    def rest_far(buf, rsem):
+        for place in (4, 6):
             arrived(buf.at[place, :, PARTS[1]], rsem.at[place, 2])
         for way in range(2):
             arrived(buf.at[6, :, HALVES[0][way]], rsem.at[6, way])
@@ -235,10 +239,10 @@
     lax.fori_loop(CAP // GROUP // 2, CAP // GROUP, prepare, 0)
     bk[CAP] = jnp.zeros((64, HALF), BF16)
 
-    def turn(buf, out, pair):
+    def turn(buf, out, pair, first, second):
         def step(i, _):
             cols = pl.ds(pl.multiple_of(i * 128, 128), 128)
-            tile = jnp.concatenate([buf[2 * pair, :, cols], buf[2 * pair + 1, :, cols]], axis=0)
+            tile = jnp.concatenate([buf[first, :, cols], buf[second, :, cols]], axis=0)
             tile = tile.T
             out[2 * i, :, pl.ds(pair * 128, 128)] = tile[:64]
             out[2 * i + 1, :, pl.ds(pair * 128, 128)] = tile[64:]
@@ -246,7 +250,8 @@
 
         lax.fori_loop(0, WIDTH // 128, step, 0, unroll=4)
 
-    def forward(lanes):
+    def forward(start, width):
+        lanes, here = pl.ds(start, width), pl.ds(0, width)
         acc[...] = jnp.zeros_like(acc)
 
         def step(i, _):
@@ -261,7 +266,7 @@
                 [jnp.concatenate([weights[0], none], axis=1), jnp.concatenate([none, weights[1]], axis=1)], axis=0
             )
             new = jnp.dot(weights, jnp.concatenate(tokens, axis=0), preferred_element_type=F32)
-            total = acc[...]
+            total = acc[:, here]
             for n, j in enumerate(slots):
                 total = new[n * 192:(n + 1) * 192] + index[KEEP_C, j].astype(F32) * total
                 gate, upper, hg = total[:64], total[64:128], total[128:]
@@ -270,12 +275,13 @@
                 hid[j, :, lanes] = (act * upper).astype(BF16)
                 gu[j, pl.ds(0, 64), lanes] = (hg * upper * sg * (1.0 + gate * (1.0 - sg))).astype(BF16)
                 gu[j, pl.ds(64, 64), lanes] = (hg * act).astype(BF16)
-            acc[...] = total
+            acc[:, here] = total
             return 0
 
         lax.fori_loop(0, CAP // 2, step, 0, unroll=4)
 
-    def backward(lanes, first_slot):
+    def backward(start, width, pairs):
+        lanes, here = pl.ds(start, width), pl.ds(0, width)
         acc_b[...] = jnp.zeros_like(acc_b)
 
         def step(i, _):
@@ -287,73 +293,96 @@
             )
             both = jnp.concatenate([gu[index[POS_R, j], :, lanes] for j in slots], axis=0)
             new = jnp.dot(weights, both, preferred_element_type=F32)
-            total = acc_b[...]
+            total = acc_b[:, here]
             for n, j in enumerate(slots):
                 total = new[n * 64:(n + 1) * 64] + index[KEEP_R, j].astype(F32) * total
-                bk[j] = total.astype(BF16)
-            acc_b[...] = total
+                bk[j, :, here] = total.astype(BF16)
+            acc_b[:, here] = total
             return 0
 
         lax.fori_loop(0, CAP // 2, step, 0, unroll=4)
 
         def place(i, _):
             cols = pl.ds(pl.multiple_of(i * 128, 128), 128)
-            both = jnp.concatenate([bk[index[LAST_R, 2 * i]], bk[index[LAST_R, 2 * i + 1]]], axis=0)
-            for q in range(2):
+            both = jnp.concatenate(
+                [bk[index[LAST_R, 2 * i], :, here], bk[index[LAST_R, 2 * i + 1], :, here]], axis=0
+            )
+            for q, (first, second) in enumerate(pairs):
                 tile = both[:, q * 128:(q + 1) * 128].T
-                part[first_slot + 2 * q, :, cols] = tile[:64]
-                part[first_slot + 2 * q + 1, :, cols] = tile[64:]
+                part[first, :, cols] = tile[:64]
+                part[second, :, cols] = tile[64:]
             return 0
 
         lax.fori_loop(0, ROWS // 2, place, 0, unroll=2)
 
-    def start_round(base, hop, rec, ssem, hsem, rsem):
-        for n in range(2):
-            here = pl.ds(n * WIDTH // 4, WIDTH // 4)
-            up, down = QUARTERS[n], QUARTERS[2 + n]
-            send(part.at[base + 2, :, up], hop.at[0, :, here], ssem.at[0, n], hsem.at[0, n], in_ring(1))
-            send(part.at[base + 2, :, down], hop.at[1, :, here], ssem.at[1, n], hsem.at[1, n], in_ring(3))
-            send(part.at[base + 1, :, down], rec.at[0, :, down], ssem.at[2, n], rsem.at[0, 2 + n], in_ring(1))
-            send(part.at[base + 3, :, up], rec.at[1, :, up], ssem.at[3, n], rsem.at[1, n], in_ring(3))
-
-    def add_round(base, n, hop, rec, ssem, hsem, rsem):
-        here = pl.ds(n * WIDTH // 4, WIDTH // 4)
-        for way, (place, step, q) in enumerate(((1, 1, n), (3, 3, 2 + n))):
-            cols = QUARTERS[q]
+    def piece(half, n, pieces):
+        return pl.ds(half * WIDTH // 2 + n * (WIDTH // 2 // pieces), WIDTH // 2 // pieces)
+
+    def start_far(base, pieces, hop, ssem, hsem):
+        for n in range(pieces):
+            for way, step in enumerate((1, 3)):
+                send(
+                    part.at[base + 2, :, piece(way, n, pieces)], hop.at[way, :, piece(0, n, pieces)],
+                    ssem.at[way, n], hsem.at[way, n], in_ring(step),
+                )
+
+    def start_near(base, pieces, rec, ssem, rsem):
+        for n in range(pieces):
+            for way, step in enumerate((1, 3)):
+                cols = piece(1 - way, n, pieces)
+                send(
+                    part.at[base + step, :, cols], rec.at[way, :, cols], ssem.at[2 + way, n],
+                    rsem.at[way, 1 - way, n], in_ring(step),
+                )
+
+    def add_round(base, n, pieces, hop, rec, ssem, hsem, rsem):
+        here = piece(0, n, pieces)
+        for way, step in enumerate((1, 3)):
+            cols = piece(way, n, pieces)
             arrived(hop.at[way, :, here], hsem.at[way, n])
-            part[base + place, :, cols] = (
-                part[base + place, :, cols].astype(F32) + hop[way, :, here].astype(F32)
+            part[base + step, :, cols] = (
+                part[base + step, :, cols].astype(F32) + hop[way, :, here].astype(F32)
             ).astype(BF16)
-            send(part.at[base + place, :, cols], rec.at[way, :, cols], ssem.at[4 + way, n], rsem.at[way, q], in_ring(step))
+            send(part.at[base + step, :, cols], rec.at[way, :, cols], ssem.at[4 + way, n], rsem.at[way, way, n], in_ring(step))
+
+    def collected(half, n, pieces, rec, rsem):
+        for way in range(2):
+            arrived(rec.at[way, :, piece(half, n, pieces)], rsem.at[way, half, n])
 
     own_in.wait()
     round_own(xc, x_send, x_recv)
     share_first(xc, x_send, x_recv)
-    turn(xc, xt, 0)
+    turn(xc, xt, 0, 0, 1)
     round_own(dc, d_send, d_recv)
     share_first(dc, d_send, d_recv)
-    turn(dc, dt, 0)
+    turn(dc, dt, 0, 0, 1)
     cross_last(xc, x_send, x_recv)
-    turn(xc, xt, 1)
+    turn(xc, xt, 1, 2, 3)
     cross_last(dc, d_send, d_recv)
-    turn(dc, dt, 1)
-    forward(pl.ds(0, HALF))
+    turn(dc, dt, 1, 2, 3)
+    forward(0, HALF)
     round_first(xc, x_send, x_recv)
     round_first(dc, d_send, d_recv)
-    backward(pl.ds(0, HALF), 0)
-    start_round(0, hop_a, rec_a, ra_send, ra_hop, ra_recv)
-
-    rest(xc, x_recv)
-    turn(xc, xt, 2)
-    turn(xc, xt, 3)
-    add_round(0, 0, hop_a, rec_a, ra_send, ra_hop, ra_recv)
-    rest(dc, d_recv)
-    turn(dc, dt, 2)
-    add_round(0, 1, hop_a, rec_a, ra_send, ra_hop, ra_recv)
-    turn(dc, dt, 3)
-    forward(pl.ds(HALF, HALF))
-    backward(pl.ds(HALF, HALF), 4)
-    start_round(4, hop_b, rec_b, rb_send, rb_hop, rb_recv)
+    backward(0, HALF, ((0, 1), (2, 3)))
+    start_far(0, PIECES_A, hop_a, ra_send, ra_hop)
+    start_near(0, PIECES_A, rec_a, ra_send, ra_recv)
+
+    rest_near(xc, x_recv)
+    turn(xc, xt, 2, 5, 7)
+    rest_near(dc, d_recv)
+    turn(dc, dt, 2, 5, 7)
+    forward(HALF, HALF // 2)
+    add_round(0, 0, PIECES_A, hop_a, rec_a, ra_send, ra_hop, ra_recv)
+    backward(HALF, HALF // 2, ((5, 7),))
+    start_near(4, PIECES_B, rec_b, rb_send, rb_recv)
+    add_round(0, 1, PIECES_A, hop_a, rec_a, ra_send, ra_hop, ra_recv)
+    rest_far(xc, x_recv)
+    turn(xc, xt, 3, 4, 6)
+    rest_far(dc, d_recv)
+    turn(dc, dt, 3, 4, 6)
+    forward(HALF + HALF // 2, HALF // 2)
+    backward(HALF + HALF // 2, HALF // 2, ((4, 6),))
+    start_far(4, PIECES_B, hop_b, rb_send, rb_hop)
 
     def grads(g, _):
         for j in range(GROUP):
@@ -376,34 +405,40 @@
             raw[rows, pl.ds(i * 128, 128)] = s1[pl.ds(i * GROUP, GROUP), :].astype(BF16)
         return 0
 
-    lax.fori_loop(0, 2, grads, 0)
-    add_round(4, 0, hop_b, rec_b, rb_send, rb_hop, rb_recv)
-    lax.fori_loop(2, 4, grads, 0)
-    add_round(4, 1, hop_b, rec_b, rb_send, rb_hop, rb_recv)
-    lax.fori_loop(4, CAP // GROUP, grads, 0)
+    def cross_sum(n):
+        for half in range(2):
+            cols = piece(half, n, PIECES_B)
+            collected(half, n, PIECES_B, rec_b, rb_recv)
+            zsum[:, cols] = (
+                part[4, :, cols].astype(F32) + rec_b[0, :, cols].astype(F32) + rec_b[1, :, cols].astype(F32)
+            ).astype(BF16)
+            send(zsum.at[:, cols], rsz.at[:, cols], z_send.at[half, n], z_recv.at[half, n], across)
+
+    for n in range(PIECES_B):
+        lax.fori_loop(n, n + 1, grads, 0)
+        add_round(4, n, PIECES_B, hop_b, rec_b, rb_send, rb_hop, rb_recv)
+    cross_sum(0)
+    lax.fori_loop(4, 5, grads, 0)
+    cross_sum(1)
+    lax.fori_loop(5, 6, grads, 0)
     blocks_out = pltpu.make_async_copy(raw, block_grads, loc.at[2])
     blocks_out.start()
-
-    for q in (0, 2, 1, 3):
-        cols = QUARTERS[q]
-        for n in range(2):
-            arrived(rec_b.at[n, :, cols], rb_recv.at[n, q])
-        zsum[:, cols] = (
-            part[4, :, cols].astype(F32) + rec_b[0, :, cols].astype(F32) + rec_b[1, :, cols].astype(F32)
-        ).astype(BF16)
-        send(zsum.at[:, cols], rsz.at[:, cols], z_send.at[q], z_recv.at[q], across)
+    cross_sum(2)
+    cross_sum(3)
+    for n in range(PIECES_A):
+        for half in range(2):
+            collected(half, n, PIECES_A, rec_a, ra_recv)
     outs = []
-    for q in (0, 2, 1, 3):
-        cols = QUARTERS[q]
-        for n in range(2):
-            arrived(rec_a.at[n, :, cols], ra_recv.at[n, q])
-        total = part[0, :, cols].astype(F32) + rec_a[0, :, cols].astype(F32) + rec_a[1, :, cols].astype(F32)
-        arrived(rsz.at[:, cols], z_recv.at[q])
-        total = total + rsz[:, cols].astype(F32)
-        ig[:, cols] = (dc[0, :, cols].astype(F32) + total).astype(BF16)
-        copy = pltpu.make_async_copy(ig.at[:, cols], input_grad.at[:, cols], loc.at[3 + q])
-        copy.start()
-        outs.append(copy)
+    for n in range(PIECES_B):
+        for half in range(2):
+            cols = piece(half, n, PIECES_B)
+            total = part[0, :, cols].astype(F32) + rec_a[0, :, cols].astype(F32) + rec_a[1, :, cols].astype(F32)
+            arrived(rsz.at[:, cols], z_recv.at[half, n])
+            total = total + rsz[:, cols].astype(F32)
+            ig[:, cols] = (dc[0, :, cols].astype(F32) + total).astype(BF16)
+            copy = pltpu.make_async_copy(ig.at[:, cols], input_grad.at[:, cols], loc.at[3 + 2 * n + half])
+            copy.start()
+            outs.append(copy)
 
     for copy in pending:
         copy.wait_send()
@@ -417,6 +452,41 @@
     blocks_out.wait()
     for copy in outs:
         copy.wait()
+
+
+def copy_kernel(a, b, a_out, b_out, a_buf, b_buf, sems):
+    pairs = [(a, a_buf, a_out, pl.ds(0, TOK))]
+    for n in range(CAP // GROUP):
+        pairs.append((b, b_buf, b_out, pl.ds(n * GROUP, GROUP)))
+    ins = [pltpu.make_async_copy(src.at[r], buf.at[r], sems.at[0, n]) for n, (src, buf, _, r) in enumerate(pairs)]
+    outs = [pltpu.make_async_copy(buf.at[r], dst.at[r], sems.at[1, n]) for n, (_, buf, dst, r) in enumerate(pairs)]
+    for copy in ins:
+        copy.start()
+    for into, out in zip(ins, outs):
+        into.wait()
+        out.start()
+    for copy in outs:
+        copy.wait()
+
+
+def hand_over(input_grad, block_grads):
+    any_space = pl.BlockSpec(memory_space=pl.ANY)
+    input_grad, block_grads = pl.pallas_call(
+        copy_kernel,
+        out_shape=(
+            jax.ShapeDtypeStruct(input_grad.shape, BF16),
+            jax.ShapeDtypeStruct(block_grads.shape, BF16),
+        ),
+        in_specs=[any_space] * 2,
+        out_specs=(any_space, any_space),
+        scratch_shapes=[
+            pltpu.VMEM(input_grad.shape, BF16),
+            pltpu.VMEM(block_grads.shape, BF16),
+            pltpu.SemaphoreType.DMA((2, 1 + CAP // GROUP)),
+        ],
+        compiler_params=pltpu.CompilerParams(vmem_limit_bytes=60 * 2**20),
+    )(input_grad, block_grads)
+    return input_grad[None], block_grads[None]
 
 
 def per_device(sections, acts, next_grad, head_grad, blocks, block_row, block_col, live):
@@ -464,21 +534,21 @@
             dma((8, 4)),
             dma((8, 4)),
             dma((2,)),
-            dma((6, 2)),
-            dma((2, 2)),
-            dma((2, 4)),
-            dma((6, 2)),
-            dma((2, 2)),
-            dma((2, 4)),
-            dma((4,)),
-            dma((4,)),
-            dma((7,)),
+            dma((6, PIECES_A)),
+            dma((2, PIECES_A)),
+            dma((2, 2, PIECES_A)),
+            dma((6, PIECES_B)),
+            dma((2, PIECES_B)),
+            dma((2, 2, PIECES_B)),
+            dma((2, PIECES_B)),
+            dma((2, PIECES_B)),
+            dma((3 + 2 * PIECES_B,)),
         ],
         compiler_params=pltpu.CompilerParams(
             collective_id=0, has_side_effects=True, vmem_limit_bytes=63 * 2**20
         ),
     )(index, acts[0], next_grad[0], head_grad, blocks[0])
-    return input_grad[None], block_grads[None]
+    return hand_over(input_grad, block_grads)
 
 
 def solution(mesh):

time: 118 us -> 112 us (0.949)
  the two profiles are of different devices: /device:TPU:39 before, /device:TPU:64 now
where the time goes in v3:
time: 112 us; the launch traced here: 111 us
  Pallas kernels  109 us (97%)
  between operations  1.45 us (1%)
    pallas_call x1, Pallas kernels, per_device(): pl.pallas_call(functools.partial(kernel, sections), out_shape=(jax.ShapeD...  105 us
    pallas_call x1, Pallas kernels, hand_over(): pl.pallas_call(copy_kernel, out_shape=(jax.ShapeDtypeStruct(input_grad.sh...  2.73 us

profile of v3, /device:TPU:64, one launch (start us, length us, event | category | flops | bytes accessed | tf_op | source)
XLA Modules:
  0.0 110.5 jit_solution(13238543026589154416)
XLA Ops:
  1.3 1.5 %shard_map.86.index = s32[16,128]{1,0:T(8,128)} custom-call(s32[1,1]{1,0:T(1,128)S(6)} %copy.9.live_ref, s32[1,96]{1,0:T(1,128)} %row_ref.1, s32[1,96]{1,0:T(1,128)} %col_ref.1), custom_call_target="tpu_custom_call" | custom-call | tf_op jit(solution)/shard_map/pallas_call | solution.py:493
  2.8 104.9 %shard_map.87 = (bf16[64,4096]{1,0:T(8,128)(2,1)}, bf16[96,12288]{1,0:T(8,128)(2,1)}) custom-call(s32[16,128]{1,0:T(8,128)} %shard_map.86.index, bf16[64,4096]{1,0:T(8,128)(2,1)} %bitcast.6, bf16[64,4096]{1,0:T(8,128)(2,1)} %bitcast.7, bf16[64,4096]{1,0:T(8,128)(2,1)} %head_grad.1, bf16[96,12288]{1,0:T(8,128)(2,1)} %bitcast.5), custom_call_target="tpu_custom_call" | custom-call | tf_op jit(solution)/shard_map/pallas_call | solution.py:501
  107.7 2.7 %shard_map.88 = (bf16[64,4096]{1,0:T(8,128)(2,1)}, bf16[96,12288]{1,0:T(8,128)(2,1)}) custom-call(bf16[64,4096]{1,0:T(8,128)(2,1)} %get-tuple-element.6.a, bf16[96,12288]{1,0:T(8,128)(2,1)} %get-tuple-element.7.b), custom_call_target="tpu_custom_call" | custom-call | tf_op jit(solution)/shard_map/pallas_call | solution.py:474

commit v4 on v3

--- a/solution.py
+++ b/solution.py
@@ -326,8 +326,8 @@
                     ssem.at[way, n], hsem.at[way, n], in_ring(step),
                 )
 
-    def start_near(base, pieces, rec, ssem, rsem):
-        for n in range(pieces):
+    def start_near(base, pieces, rec, ssem, rsem, first=0, end=None):
+        for n in range(first, pieces if end is None else end):
             for way, step in enumerate((1, 3)):
                 cols = piece(1 - way, n, pieces)
                 send(
@@ -362,10 +362,10 @@
     turn(dc, dt, 1, 2, 3)
     forward(0, HALF)
     round_first(xc, x_send, x_recv)
+    backward(0, HALF, ((0, 1), (2, 3)))
     round_first(dc, d_send, d_recv)
-    backward(0, HALF, ((0, 1), (2, 3)))
     start_far(0, PIECES_A, hop_a, ra_send, ra_hop)
-    start_near(0, PIECES_A, rec_a, ra_send, ra_recv)
+    start_near(0, PIECES_A, rec_a, ra_send, ra_recv, 0, 1)
 
     rest_near(xc, x_recv)
     turn(xc, xt, 2, 5, 7)
@@ -417,6 +417,7 @@
     for n in range(PIECES_B):
         lax.fori_loop(n, n + 1, grads, 0)
         add_round(4, n, PIECES_B, hop_b, rec_b, rb_send, rb_hop, rb_recv)
+    start_near(0, PIECES_A, rec_a, ra_send, ra_recv, 1)
     cross_sum(0)
     lax.fori_loop(4, 5, grads, 0)
     cross_sum(1)

time: 112 us -> 113 us (level)
  no operation moved by 1% of the time
where the time goes in v4:
time: 113 us; the launch traced here: 111 us
  Pallas kernels  109 us (96%)
  between operations  1.45 us (1%)
    pallas_call x1, Pallas kernels, per_device(): pl.pallas_call(functools.partial(kernel, sections), out_shape=(jax.ShapeD...  105 us
    pallas_call x1, Pallas kernels, hand_over(): pl.pallas_call(copy_kernel, out_shape=(jax.ShapeDtypeStruct(input_grad.sh...  2.73 us

profile of v4, /device:TPU:64, one launch (start us, length us, event | category | flops | bytes accessed | tf_op | source)
XLA Modules:
  0.0 110.5 jit_solution(6887756905974715576)
XLA Ops:
  1.3 1.5 %shard_map.86.index = s32[16,128]{1,0:T(8,128)} custom-call(s32[1,1]{1,0:T(1,128)S(6)} %copy.9.live_ref, s32[1,96]{1,0:T(1,128)} %row_ref.1, s32[1,96]{1,0:T(1,128)} %col_ref.1), custom_call_target="tpu_custom_call" | custom-call | tf_op jit(solution)/shard_map/pallas_call | solution.py:494
  2.8 104.9 %shard_map.87 = (bf16[64,4096]{1,0:T(8,128)(2,1)}, bf16[96,12288]{1,0:T(8,128)(2,1)}) custom-call(s32[16,128]{1,0:T(8,128)} %shard_map.86.index, bf16[64,4096]{1,0:T(8,128)(2,1)} %bitcast.6, bf16[64,4096]{1,0:T(8,128)(2,1)} %bitcast.7, bf16[64,4096]{1,0:T(8,128)(2,1)} %head_grad.1, bf16[96,12288]{1,0:T(8,128)(2,1)} %bitcast.5), custom_call_target="tpu_custom_call" | custom-call | tf_op jit(solution)/shard_map/pallas_call | solution.py:502
  107.7 2.7 %shard_map.88 = (bf16[64,4096]{1,0:T(8,128)(2,1)}, bf16[96,12288]{1,0:T(8,128)(2,1)}) custom-call(bf16[64,4096]{1,0:T(8,128)(2,1)} %get-tuple-element.6.a, bf16[96,12288]{1,0:T(8,128)(2,1)} %get-tuple-element.7.b), custom_call_target="tpu_custom_call" | custom-call | tf_op jit(solution)/shard_map/pallas_call | solution.py:475

commit v5 on v4

--- a/solution.py
+++ b/solution.py
@@ -278,7 +278,7 @@
             acc[:, here] = total
             return 0
 
-        lax.fori_loop(0, CAP // 2, step, 0, unroll=4)
+        lax.fori_loop(0, CAP // 2, step, 0, unroll=4 * HALF // width)
 
     def backward(start, width, pairs):
         lanes, here = pl.ds(start, width), pl.ds(0, width)
@@ -300,7 +300,7 @@
             acc_b[:, here] = total
             return 0
 
-        lax.fori_loop(0, CAP // 2, step, 0, unroll=4)
+        lax.fori_loop(0, CAP // 2, step, 0, unroll=4 * HALF // width)
 
         def place(i, _):
             cols = pl.ds(pl.multiple_of(i * 128, 128), 128)

time: 113 us -> 109 us (0.965); the launches traced: 111 us -> 109 us
  Pallas kernels: 109 us -> 107 us
    pallas_call x1, Pallas kernels: 105 us -> 103 us  [per_device(): pl.pallas_call(functools.partial(kernel, sections), out_shape=(jax.ShapeD...]
where the time goes in v5:
time: 109 us
  Pallas kernels  107 us (98%)
  between operations  1.45 us (1%)
    pallas_call x1, Pallas kernels, per_device(): pl.pallas_call(functools.partial(kernel, sections), out_shape=(jax.ShapeD...  103 us
    pallas_call x1, Pallas kernels, hand_over(): pl.pallas_call(copy_kernel, out_shape=(jax.ShapeDtypeStruct(input_grad.sh...  2.73 us

profile of v5, /device:TPU:64, one launch (start us, length us, event | category | flops | bytes accessed | tf_op | source)
XLA Modules:
  0.0 108.6 jit_solution(11569455929605843725)
XLA Ops:
  1.3 1.5 %shard_map.86.index = s32[16,128]{1,0:T(8,128)} custom-call(s32[1,1]{1,0:T(1,128)S(6)} %copy.9.live_ref, s32[1,96]{1,0:T(1,128)} %row_ref.1, s32[1,96]{1,0:T(1,128)} %col_ref.1), custom_call_target="tpu_custom_call" | custom-call | tf_op jit(solution)/shard_map/pallas_call | solution.py:494
  2.8 102.9 %shard_map.87 = (bf16[64,4096]{1,0:T(8,128)(2,1)}, bf16[96,12288]{1,0:T(8,128)(2,1)}) custom-call(s32[16,128]{1,0:T(8,128)} %shard_map.86.index, bf16[64,4096]{1,0:T(8,128)(2,1)} %bitcast.6, bf16[64,4096]{1,0:T(8,128)(2,1)} %bitcast.7, bf16[64,4096]{1,0:T(8,128)(2,1)} %head_grad.1, bf16[96,12288]{1,0:T(8,128)(2,1)} %bitcast.5), custom_call_target="tpu_custom_call" | custom-call | tf_op jit(solution)/shard_map/pallas_call | solution.py:502
  105.7 2.7 %shard_map.88 = (bf16[64,4096]{1,0:T(8,128)(2,1)}, bf16[96,12288]{1,0:T(8,128)(2,1)}) custom-call(bf16[64,4096]{1,0:T(8,128)(2,1)} %get-tuple-element.6.a, bf16[96,12288]{1,0:T(8,128)(2,1)} %get-tuple-element.7.b), custom_call_target="tpu_custom_call" | custom-call | tf_op jit(solution)/shard_map/pallas_call | solution.py:475
